TPU v7x, 32 devices: a whole 2x2x4 slice. The times are simulated.
32 devices in a mesh: dp: 16 (over z, y, x), mp: 2 (over core).
Axes of the slice: x: 2, y: 2, z: 4, core: 2. Of those that a mesh axis runs over, the one named last changes fastest.
Arguments:
- tokens: bfloat16 [18464, 768], P('dp'), may hold values from -6 to 6
- row_ids: int32 [18464], P('dp'), may hold values from 0 to 31, as said below
- select: int32 [18464], P('dp'), may hold values 0 or 1
- priority: int32 [18464], P('dp'), may hold values from 0 to 1153, as said below
- first_gain: float32 [768], replicated, may hold values from 0.5 to 1.5
- first_shift: float32 [768], replicated, may hold values from -1 to 1
- router: float32 [768], replicated, may hold values from -0.21875 to 0.21875
- w_attend: bfloat16 [768, 3, 768], P(None, None, 'mp'), may hold values from -0.21875 to 0.21875
- w_output: bfloat16 [768, 768], P('mp'), may hold values from -3 to 3
- second_gain: float32 [768], replicated, may hold values from 0.5 to 1.5
- second_shift: float32 [768], replicated, may hold values from -1 to 1
- w_expand: bfloat16 [768, 3072], P(None, 'mp'), may hold values from -0.21875 to 0.21875
- w_reduce: bfloat16 [3072, 768], P('mp'), may hold values from -0.109375 to 0.109375
- cotangent: bfloat16 [18464, 768], P('dp'), may hold values from -6 to 6
Outputs:
- layer_out: bfloat16 [18464, 768], P('dp')
- tokens_grad: float32 [18464, 768], P('dp')
- first_gain_grad: float32 [768], P('dp')
- first_shift_grad: float32 [768], P('dp')
- router_grad: float32 [768], P('dp')
- attend_grad: float32 [768, 3, 768], P('dp', None, 'mp')
- output_grad: float32 [768, 768], P('mp', 'dp')
- second_gain_grad: float32 [768], P('dp')
- second_shift_grad: float32 [768], P('dp')
- expand_grad: float32 [768, 3072], P('dp', 'mp')
- reduce_grad: float32 [3072, 768], P('mp', 'dp')
Inputs may be any that keep to these rules, and one draw needn't show every extreme that they name: `row_ids`: each of the 32 rows has 577 tokens, and every index of dp holds 36 or one more of every row's tokens. `priority`: on each index of dp the 1154 values are a permutation.
All inputs are finite; a program needn't handle non-finite values. No bound on the sum of `select` on one device may be relied on, other than what follows from the above.
Results may differ from a plain program's by a relative error of at most 0.015.
Values may be sent and summed in bfloat16 or wider, within the bound.
A program may use at most 192 MiB of HBM per device.

v0:
```python
import functools

import jax
import jax.numpy as jnp
from jax import lax
from jax.experimental import pallas as pl
from jax.experimental.pallas import tpu as pltpu
from jax.sharding import PartitionSpec as P

HD = 64
ROW_LEN = 577
EPSILON = 1e-06
MASKED_SCORE = -1000000000.0
EMPTY = 1e30
WINDOW = 3
BF = jnp.bfloat16
F32 = jnp.float32
MESH = pl.DeviceIdType.MESH


def mm(a, b, dims):
    return lax.dot_general(a, b, (dims, ((), ())), preferred_element_type=F32)


def norm_stats(value):
    center = value - jnp.mean(value, axis=-1, keepdims=True)
    inv = lax.rsqrt(jnp.mean(center * center, axis=-1, keepdims=True) + EPSILON)
    return center * inv, inv


def norm_pull(e, nhat, inv):
    return (e - jnp.mean(e, axis=-1, keepdims=True) - nhat * jnp.mean(e * nhat, axis=-1, keepdims=True)) * inv


def swap(value):
    return lax.ppermute(value, "mp", [(0, 1), (1, 0)])


def scatter_sum(grad, order):
    count = lax.axis_size("dp")
    me = lax.axis_index("dp")
    bits = count.bit_length() - 1
    width = grad.shape[0] // count
    dims = [2] * bits
    value = grad.reshape(dims + [width, grad.shape[1]])
    out = None
    for step in order:
        axis = bits - 1 - step
        mine = (me >> step) & 1
        give = lax.dynamic_slice_in_dim(value, 1 - mine, 1, axis)
        keep = lax.dynamic_slice_in_dim(value, mine, 1, axis)
        got = lax.ppermute(give, "dp", [(i, i ^ (1 << step)) for i in range(count)])
        out = keep.astype(F32) + got.astype(F32)
        value = out.astype(grad.dtype)
    return out.reshape(width, grad.shape[1])


def block_plan(capacity, width):
    whole = capacity // 16 * 16
    left = capacity - whole
    parts = max(s for s in (1, 2, 3, 6) if left * s <= 16 and width % (128 * s) == 0)
    return whole, left, parts


def rest_map(peers, left, parts):
    at = jnp.arange(peers * 16)[None, :, None]
    row = jnp.arange(peers * left)[None, None, :]
    part = jnp.arange(parts)[:, None, None]
    return ((at // 16 == row // left) & (at % 16 == part * left + row % left)).astype(BF)


def greet(peers, with_pair=False):
    me, core = lax.axis_index("dp"), lax.axis_index("mp")
    barrier = pltpu.get_barrier_semaphore()

    def hello(d, carry):
        pl.semaphore_signal(
            barrier, inc=1, device_id=(lax.rem(me + d, peers), core), device_id_type=MESH
        )
        return carry

    lax.fori_loop(1, peers, hello, 0)
    if with_pair:
        pl.semaphore_signal(barrier, inc=1, device_id=(me, 1 - core), device_id_type=MESH)
    pl.semaphore_wait(barrier, peers if with_pair else peers - 1)


def pack(value, blocks, maps, whole):
    rest = blocks[-1]
    peers, lanes = rest.shape[0], rest.shape[2]
    if whole:
        blocks[0][...] = value[: peers * whole].reshape(peers, whole, value.shape[1])
    tail = value[peers * whole :]
    total = sum(
        mm(maps[i], tail[:, i * lanes : (i + 1) * lanes], ((1,), (0,)))
        for i in range(maps.shape[0])
    )
    rest[...] = total.astype(BF).reshape(peers, 16, lanes)


def unpack(blocks, maps, whole, out):
    rest = blocks[-1]
    peers, lanes = rest.shape[0], rest.shape[2]
    if whole:
        out[: peers * whole, :] = blocks[0][...].reshape(peers * whole, out.shape[1])
    left = rest[...].reshape(peers * 16, lanes)
    for i in range(maps.shape[0]):
        out[peers * whole :, i * lanes : (i + 1) * lanes] = mm(
            maps[i], left, ((0,), (0,))
        ).astype(BF)


def copies(d, pairs, sends, recvs, back=False):
    me, core = lax.axis_index("dp"), lax.axis_index("mp")
    peers = pairs[0][0].shape[0]
    to, source = lax.rem(me + d, peers), lax.rem(me + peers - d, peers)
    return [
        pltpu.make_async_remote_copy(
            src_ref=here.at[to],
            dst_ref=there.at[source if back else me],
            send_sem=sends.at[i, d],
            recv_sem=recvs.at[i, d],
            device_id=(to, core),
            device_id_type=MESH,
        )
        for i, (here, there) in enumerate(pairs)
    ]


def send_all(pairs, sends, recvs):
    me = lax.axis_index("dp")

    def start(d, carry):
        for copy in copies(d, pairs, sends, recvs):
            copy.start()
        return carry

    lax.fori_loop(1, pairs[0][0].shape[0], start, 0)
    for here, there in pairs:
        there[pl.ds(me, 1)] = here[pl.ds(me, 1)]


def wait_all(pairs, sends, recvs):
    def finish(d, carry):
        for copy in copies(d, pairs, sends, recvs, back=True):
            copy.wait_recv()
        return carry

    def drain(d, carry):
        for copy in copies(d, pairs, sends, recvs):
            copy.wait_send()
        return carry

    lax.fori_loop(1, pairs[0][0].shape[0], finish, 0)
    lax.fori_loop(1, pairs[0][0].shape[0], drain, 0)


def lane_masks():
    low = lax.broadcasted_iota(jnp.int32, (1, 128), 1) < HD
    return low, jnp.logical_not(low)


def attend_kernel(
    whole, normed, maps, w_own, w_other, gathered, buffer, proj, probs,
    w_vmem, context, key_mask, w_sem, send_1, recv_1, send_2, recv_2, *blocks,
):
    core = lax.axis_index("mp")
    loads = [
        pltpu.make_async_copy(w, w_vmem.at[i], w_sem.at[i]) for i, w in enumerate((w_own, w_other))
    ]
    for load in loads:
        load.start()
    given_1, taken_1, given_2, taken_2 = split_blocks(blocks)
    pack(normed[...], given_1, maps, whole)
    greet(given_1[-1].shape[0])
    first = list(zip(given_1, taken_1))
    send_all(first, send_1, recv_1)
    wait_all(first, send_1, recv_1)
    unpack(taken_1, maps, whole, buffer)
    pick = (lax.broadcasted_iota(jnp.int32, (8, 128), 1) == 0).astype(BF)
    key_mask[...] = jnp.where(
        mm(pick, buffer[:, :128], ((1,), (1,))) < 0.5 * EMPTY, 1.0, 0.0
    )
    received = buffer[...].astype(F32)
    buffer[...] = jnp.where(received[:, :1] < 0.5 * EMPTY, received, 0.0).astype(BF)
    cols = w_own.shape[2]
    pairs = cols // 128
    masks = lane_masks()
    zero = jnp.zeros((), BF)
    for i in range(2):
        loads[i].wait()
        for which in range(3):
            proj[i, :, which * cols : (which + 1) * cols] = mm(
                buffer[...], w_vmem[i, which], ((1,), (0,))
            ).astype(BF)
        canonical = core if i == 0 else 1 - core

        def pair_step(p, carry, i=i, canonical=canonical):
            def part(which):
                return proj[i, :, pl.ds(pl.multiple_of(which * cols + p * 128, 128), 128)]

            q, k, v = part(0), part(1), part(2)
            total = 0.0
            for e, lanes in enumerate(masks):
                scores = mm(q, jnp.where(lanes, k, zero), ((1,), (1,))) * HD ** (-0.5)
                scores = jnp.where(key_mask[:1, :] > 0.5, scores, MASKED_SCORE)
                weights = jnp.exp(scores - jnp.max(scores, axis=-1, keepdims=True))
                low = (weights * (1.0 / jnp.sum(weights, axis=-1, keepdims=True))).astype(BF)
                probs[(i * pairs + p) * 2 + e] = low
                total = total + mm(low, jnp.where(lanes, v, zero), ((1,), (0,)))
            context[:, pl.ds(pl.multiple_of(canonical * cols + p * 128, 128), 128)] = total.astype(BF)
            return carry

        lax.fori_loop(0, pairs, pair_step, 0)
    pack(context[...], given_2, maps, whole)
    second = list(zip(given_2, taken_2))
    send_all(second, send_2, recv_2)
    wait_all(second, send_2, recv_2)
    unpack(taken_2, maps, whole, gathered)


class Halving:
    def __init__(self, source, bufs, sends, recvs, order, out):
        self.source, self.bufs, self.sends, self.recvs = source, bufs, sends, recvs
        self.order, self.out = order, out
        self.stages = len(order)
        self.rows = bufs[0].shape[1]
        self.counts = [buf.shape[0] for buf in bufs]
        self.first = [k for stage, k in halving_plan(self.stages) if stage == 0]

    def bit(self, stage):
        return lax.rem(lax.div(lax.axis_index("dp"), 1 << self.order[stage]), 2)

    def block(self, k, kept):
        index = 0
        for stage in range(self.stages):
            mine = self.bit(stage)
            if stage == 0:
                value = mine if kept else 1 - mine
            else:
                part = lax.rem(lax.div(k, self.counts[stage]), 2)
                value = (1 - mine) * (1 - part) + mine * part
            index = index + value * (1 << self.order[stage])
        return pl.ds(pl.multiple_of(index * self.rows, 16), self.rows)

    def copy(self, stage, k):
        me, core = lax.axis_index("dp"), lax.axis_index("mp")
        to = me + (1 - 2 * self.bit(stage)) * (1 << self.order[stage])
        at = sum(self.counts[:stage]) + k
        src = self.source.at[self.block(k, False), :] if stage == 0 else self.bufs[stage - 1].at[k]
        return pltpu.make_async_remote_copy(
            src_ref=src,
            dst_ref=self.bufs[stage].at[k],
            send_sem=self.sends.at[at],
            recv_sem=self.recvs.at[at],
            device_id=(to, core),
            device_id_type=MESH,
        )

    def begin(self):
        for k in self.first[:WINDOW]:
            self.copy(0, k).start()

    def step(self, stage, k):
        self.copy(stage, k).wait_recv()
        buf = self.bufs[stage]
        if stage == 0:
            own = self.source[self.block(k, True), :]
        else:
            own = self.bufs[stage - 1][pl.ds(self.counts[stage] + k, 1)][0]
        total = own.astype(F32) + buf[pl.ds(k, 1)][0].astype(F32)
        if stage == self.stages - 1:
            self.out[...] = total
            return
        buf[pl.ds(k, 1)] = total.astype(BF)[None]
        if k < self.counts[stage + 1]:
            self.copy(stage + 1, k).start()
        if stage == 0:
            ahead = self.first.index(k) + WINDOW
            if ahead < len(self.first):
                self.copy(0, self.first[ahead]).start()

    def drain(self):
        for stage, count in enumerate(self.counts):

            def finish(k, carry, stage=stage):
                self.copy(stage, k).wait_send()
                return carry

            lax.fori_loop(0, count, finish, 0)


def halving_plan(stages):
    counts = [1 << (stages - 1 - stage) for stage in range(stages)]
    times = {}
    for stage, count in enumerate(counts):
        for k in range(count):
            if stage == 0:
                bits = [(k >> i) & 1 for i in range(stages - 1)]
                times[stage, k] = 1 + sum(bit << (stages - 2 - i) for i, bit in enumerate(bits))
            else:
                times[stage, k] = 1.6 + max(times[stage - 1, k], times[stage - 1, count + k])
    return sorted(times, key=lambda key: (times[key], key))


def advance(chains, steps):
    for stage, k in steps:
        for chain in chains:
            chain.step(stage, k)


def back_kernel(
    whole, orders, context_grad, maps, mask, logit_grad, second_sums, gain, shift, router, place, want,
    act_in, pre_in, w_own, w_other, proj_in, probs_in,
    buffer_in, attended_in, gathered_in, hidden_in, ct_in, x_in, mixed_in, layer_in,
    expand_out, reduce_out, late_out, layer_out, tokens_out, sums_out,
    act, pre_grad, w_vmem, proj, probs, upstream, proj_grad, total_grad,
    expand_give, reduce_give, expand_got, reduce_got, expand_acc, reduce_acc, sums, sums_got, layer_stage, tokens_stage, out_sem,
    buffer, attended_grad, gathered, hidden_t, ct_t, x, mixed_grad, layer_own,
    load_sem, pair_send, pair_recv, sums_send, sums_recv, free_sem, send_1, recv_1, send_2, recv_2, *rest,
):
    dp, core = lax.axis_index("dp"), lax.axis_index("mp")
    peers = lax.axis_size("dp")
    width, columns = expand_give.shape
    slots = buffer.shape[0]
    count = x.shape[0]
    late_give, late_got = act.at[pl.ds(0, width), :], pre_grad.at[pl.ds(0, width), :]
    late_acc = expand_give
    if orders is None:
        expand_acc, reduce_acc, late_acc = expand_out, reduce_out, late_out
    own, other = pl.ds(0, count), pl.ds(count, count)
    local = [
        (hidden_in, hidden_t),
        (pre_in.at[1], pre_grad.at[other, :]),
        (pre_in.at[0], pre_grad.at[own, :]),
        (ct_in, ct_t),
        (act_in.at[1], act.at[other, :]),
        (act_in.at[0], act.at[own, :]),
        (attended_in, attended_grad),
        (gathered_in, gathered),
        (proj_in, proj),
        (probs_in, probs),
        (w_own, w_vmem.at[0]),
        (w_other, w_vmem.at[1]),
        (buffer_in, buffer),
        (layer_in, layer_own),
        (x_in, x),
        (mixed_in, mixed_grad),
    ]
    loads = [
        pltpu.make_async_copy(here, there, load_sem.at[i]) for i, (here, there) in enumerate(local)
    ]
    for load in loads:
        load.start()
    kinds = 2 if whole else 1
    given_1, taken_1, given_2, taken_2 = split_blocks(rest[: 4 * kinds])
    rest = rest[4 * kinds :]
    half = columns // 2
    left_half, right_half = pl.ds(0, half), pl.ds(half, half)
    chains = []
    stages = 0
    if orders is not None:
        stages = len(orders[0])
        kinds_of = (
            (expand_acc, expand_out, orders[0]),
            (reduce_acc, reduce_out, orders[1]),
            (late_acc.at[:, left_half], late_out.at[:, left_half], orders[0]),
            (late_acc.at[:, right_half], late_out.at[:, right_half], orders[1]),
        )
        for i, (source, out, order) in enumerate(kinds_of):
            mine = rest[i * (stages + 2) : (i + 1) * (stages + 2)]
            chains.append(Halving(source, mine[2:], mine[0], mine[1], order, out))

    pack(context_grad[...], given_1, maps, whole)
    greet(peers, with_pair=True)
    first = list(zip(given_1, taken_1))
    send_all(first, send_1, recv_1)

    def pair_copy(at, give, got):
        return pltpu.make_async_remote_copy(
            src_ref=give,
            dst_ref=got,
            send_sem=pair_send.at[at],
            recv_sem=pair_recv.at[at],
            device_id=(dp, 1 - core),
            device_id_type=MESH,
        )

    chunk = 512 if columns % 512 == 0 else columns
    steps = columns // chunk

    def at(j):
        return pl.ds(pl.multiple_of(j * chunk, 128), chunk)

    weights = (
        (hidden_t, pre_grad, expand_give, expand_got, expand_acc),
        (ct_t, act, reduce_give, reduce_got, reduce_acc),
    )

    def weight_copy(i, j):
        give, got = weights[i][2:4]
        return pair_copy(i * steps + j, give.at[:, at(j)], got.at[:, at(j)])

    for i, (left, right, give, got, acc) in enumerate(weights):
        loads[3 * i].wait()
        loads[3 * i + 1].wait()

        def other_part(j, carry, i=i, left=left, right=right, give=give):
            give[:, at(j)] = mm(left[...], right[other, at(j)], ((1,), (0,))).astype(BF)
            weight_copy(i, j).start()
            return carry

        def own_part(j, carry, i=i, left=left, right=right, got=got, acc=acc):
            value = mm(left[...], right[own, at(j)], ((1,), (0,)))
            weight_copy(i, j).wait_recv()
            acc[:, at(j)] = (value + got[:, at(j)].astype(F32)).astype(BF)
            return carry

        lax.fori_loop(0, steps, other_part, 0)
        loads[3 * i + 2].wait()
        lax.fori_loop(0, steps, own_part, 0)
        if chains:
            chains[i].begin()
    pl.semaphore_signal(free_sem, inc=1, device_id=(dp, 1 - core), device_id_type=MESH)
    for i in range(2):

        def sent(j, carry, i=i):
            weight_copy(i, j).wait_send()
            return carry

        lax.fori_loop(0, steps, sent, 0)
    cols = w_own.shape[2]
    attend_cols = 3 * cols
    own_cols = pl.ds(pl.multiple_of(core * cols, 128), cols)
    other_cols = pl.ds(pl.multiple_of((1 - core) * cols, 128), cols)
    loads[6].wait()
    loads[7].wait()
    late_give[:, attend_cols:] = mm(
        attended_grad[...], gathered[:, other_cols], ((0,), (0,))
    ).astype(BF)
    late_acc[:, attend_cols:] = mm(attended_grad[...], gathered[:, own_cols], ((0,), (0,))).astype(BF)
    pl.semaphore_wait(free_sem, 1)

    wait_all(first, send_1, recv_1)
    unpack(taken_1, maps, whole, upstream)
    for load in loads[8:]:
        load.wait()
    pairs = cols // 128
    masks = lane_masks()
    zero = jnp.zeros((), BF)
    for i in range(2):
        canonical = core if i == 0 else 1 - core

        def pair_step(p, carry, i=i, canonical=canonical):
            def place_of(which):
                return pl.ds(pl.multiple_of(which * cols + p * 128, 128), 128)

            q, k, v = (proj[i, :, place_of(which)] for which in range(3))
            up = upstream[:, place_of(canonical)]
            q_grad = k_grad = v_grad = 0.0
            for e, lanes in enumerate(masks):
                low = probs[(i * pairs + p) * 2 + e]
                wide = low.astype(F32)
                probs_grad = mm(up, jnp.where(lanes, v, zero), ((1,), (1,)))
                delta = jnp.sum(wide * probs_grad, axis=-1, keepdims=True)
                scores_grad = (wide * (probs_grad - delta)).astype(BF)
                v_grad = v_grad + mm(low, jnp.where(lanes, up, zero), ((0,), (0,)))
                q_grad = q_grad + mm(scores_grad, jnp.where(lanes, k, zero), ((1,), (0,)))
                k_grad = k_grad + mm(scores_grad, jnp.where(lanes, q, zero), ((0,), (0,)))
            proj_grad[i, :, place_of(0)] = (q_grad * HD ** (-0.5)).astype(BF)
            proj_grad[i, :, place_of(1)] = (k_grad * HD ** (-0.5)).astype(BF)
            proj_grad[i, :, place_of(2)] = v_grad.astype(BF)
            return carry

        lax.fori_loop(0, pairs, pair_step, 0)
    total_grad[...] = sum(
        mm(proj_grad[i, :, which * cols : (which + 1) * cols], w_vmem[i, which], ((1,), (1,)))
        for i in range(2)
        for which in range(3)
    ).astype(BF)
    pack(total_grad[...], given_2, maps, whole)
    second = list(zip(given_2, taken_2))
    send_all(second, send_2, recv_2)

    base = 2 * steps
    late_copy = [
        pair_copy(base + j, late_give.at[:, part], late_got.at[:, part])
        for j, part in enumerate((left_half, right_half))
    ]
    def attend_at(which):
        return pl.ds(pl.multiple_of(which * cols, 128), cols)

    def late_other(which, carry):
        value = mm(buffer[...], proj_grad[1, :, attend_at(which)], ((0,), (0,)))
        act[pl.ds(0, width), attend_at(which)] = value.astype(BF)
        return carry

    def late_own(which, carry):
        value = mm(buffer[...], proj_grad[0, :, attend_at(which)], ((0,), (0,)))
        got = pre_grad[pl.ds(0, width), attend_at(which)].astype(F32)
        late_acc[:, attend_at(which)] = (value + got).astype(BF)
        return carry

    lax.fori_loop(0, 3, late_other, 0)
    for copy in late_copy:
        copy.start()
    for copy in late_copy:
        copy.wait_recv()
    lax.fori_loop(0, 3, late_own, 0)
    late_acc[:, attend_cols:] = (
        late_acc[:, attend_cols:].astype(F32) + late_got[:, attend_cols:].astype(F32)
    ).astype(BF)
    for chain in chains[2:]:
        chain.begin()
    layer_copy = pair_copy(
        base + 2, layer_own, reduce_got.at[pl.ds(0, count), pl.ds(0, width)]
    )
    layer_copy.start()
    steps_left = halving_plan(stages) if chains else []
    cuts = [len(steps_left) * part // 15 for part in (5, 10, 13, 15)]
    advance(chains[:2], steps_left[: cuts[0]])

    wait_all(second, send_2, recv_2)
    unpack(taken_2, maps, whole, upstream)
    step_rows = 32
    tokens_own = reduce_give.at[pl.ds(0, count), pl.ds(0, width)]
    tokens_got = expand_got.at[pl.ds(0, count), pl.ds(0, width)]

    def norm_rows(r, carry, kept):
        rows = pl.ds(pl.multiple_of(r * step_rows, step_rows), step_rows)
        normal, scale = norm_stats(x[rows, :].astype(F32))
        normed = (normal * gain[...] + shift[...]).astype(BF).astype(F32)
        logit = logit_grad[rows, :]
        grad = logit * router[...]
        if kept:
            grad = grad + jnp.where(mask[rows, :] > 0.5, upstream[rows, :].astype(F32), 0.0)
        total = mixed_grad[rows, :] + norm_pull(grad * gain[...], normal, scale)
        reduce_give[rows, pl.ds(0, width)] = total.astype(BF)
        return (
            carry[0] + row_sums(grad * normal),
            carry[1] + row_sums(grad),
            carry[2] + row_sums(logit * normed),
        )

    zeros = jnp.zeros((8, width), F32)
    carry = (zeros, zeros, zeros)
    kept_steps = slots // step_rows
    carry = lax.fori_loop(0, kept_steps, functools.partial(norm_rows, kept=True), carry)
    carry = lax.fori_loop(
        kept_steps, count // step_rows, functools.partial(norm_rows, kept=False), carry
    )
    tokens_copy = pair_copy(base + 3, tokens_own, tokens_got)
    tokens_copy.start()
    for i in range(3):
        sums[0, i : i + 1, :] = jnp.sum(carry[i], axis=0, keepdims=True)
    sums[0, 3:5, :] = second_sums[...]
    sums[0, 5:8, :] = jnp.zeros((3, width), F32)

    def sums_copy(stage):
        if stage < sums_got.shape[0] - 1:
            bit = lax.rem(lax.div(dp, 1 << stage), 2)
            to = (dp + (1 - 2 * bit) * (1 << stage), core)
        else:
            to = (dp, 1 - core)
        return pltpu.make_async_remote_copy(
            src_ref=sums.at[stage],
            dst_ref=sums_got.at[stage],
            send_sem=sums_send.at[stage],
            recv_sem=sums_recv.at[stage],
            device_id=to,
            device_id_type=MESH,
        )

    sums_stages = sums_got.shape[0]
    sums_copy(0).start()

    def sums_step(stage):
        sums_copy(stage).wait_recv()
        total = sums[stage] + sums_got[stage]
        if stage + 1 < sums_stages:
            sums[stage + 1] = total
            sums_copy(stage + 1).start()
        else:
            sums_out[...] = total

    def unpick(own, other, out, stage, sems):
        total = out.shape[0]
        block = stage.shape[1]
        full = total // block
        tail = total - full * block

        def out_copy(r, size):
            slot = lax.rem(r, 2)
            rows = pl.ds(pl.multiple_of(r * block, block), size)
            return pltpu.make_async_copy(
                stage.at[slot, pl.ds(0, size), :], out.at[rows, :], sems.at[slot]
            )

        def emit(r, size):
            rows = pl.ds(pl.multiple_of(r * block, block), size)
            hit = (place[rows, :] == want[...]).astype(F32).astype(BF)
            value = mm(hit[:, :count], own[...], ((1,), (0,))) + mm(
                hit[:, count:], other[...], ((1,), (0,))
            )
            stage[lax.rem(r, 2), pl.ds(0, size), :] = value.astype(out.dtype)
            out_copy(r, size).start()

        def body(r, carry):
            @pl.when(r >= 2)
            def _():
                out_copy(r - 2, block).wait()

            emit(r, block)
            return carry

        lax.fori_loop(0, full, body, 0)
        if tail:
            out_copy(full - 2, block).wait()
            emit(full, tail)
            out_copy(full - 1, block).wait()
            out_copy(full, tail).wait()
        else:
            out_copy(full - 2, block).wait()
            out_copy(full - 1, block).wait()

    advance(chains[:2], steps_left[cuts[0] : cuts[1]])
    layer_copy.wait_recv()
    layer_got = reduce_got.at[pl.ds(0, count), pl.ds(0, width)]
    unpick(layer_own, layer_got, layer_out, layer_stage, out_sem.at[0])
    sums_step(0)
    advance(chains[:2], steps_left[cuts[1] : cuts[2]])
    sums_step(1)
    tokens_copy.wait_recv()
    unpick(tokens_own, tokens_got, tokens_out, tokens_stage, out_sem.at[1])
    sums_step(2)
    advance(chains[:2], steps_left[cuts[2] :])
    for stage in range(3, sums_stages):
        sums_step(stage)
    advance(chains[2:], steps_left)
    for chain in chains:
        chain.drain()
    for copy in (*late_copy, layer_copy, tokens_copy):
        copy.wait_send()
    for stage in range(sums_stages):
        sums_copy(stage).wait_send()


def split_blocks(blocks):
    step = len(blocks) // 4
    return [blocks[i * step : (i + 1) * step] for i in range(4)]


def block_scratch(peers, whole, left, parts, width):
    shapes = [(peers, whole, width)] if whole else []
    shapes.append((peers, 16, width // parts))
    return [pltpu.VMEM(shape, BF) for _ in range(4) for shape in shapes], len(shapes)


def exchange_call(
    kernel, name, collective_id, capacity, args, spaces, outs, scratch, after=(), out_spaces=None
):
    width = args[0].shape[1]
    peers = lax.axis_size("dp")
    whole, left, parts = block_plan(capacity, width)
    blocks, kinds = block_scratch(peers, whole, left, parts, width)
    return pl.pallas_call(
        functools.partial(kernel, whole),
        out_shape=[jax.ShapeDtypeStruct(*out) for out in outs],
        in_specs=[pl.BlockSpec(memory_space=space) for space in spaces],
        out_specs=[
            pl.BlockSpec(memory_space=space) for space in out_spaces or [pltpu.VMEM] * len(outs)
        ],
        scratch_shapes=[
            *scratch,
            *[pltpu.SemaphoreType.DMA((kinds, peers))] * 4,
            *blocks,
            *after,
        ],
        compiler_params=pltpu.CompilerParams(
            collective_id=collective_id, has_side_effects=True, vmem_limit_bytes=58 * 2**20
        ),
        name=name,
    )(*args)


def attend(normed, maps, w_own, w_other, capacity):
    slots, width = normed.shape
    columns = 3 * w_own.shape[2]
    heads = 2 * columns // 3 // HD
    return exchange_call(
        attend_kernel, "attend", 0, capacity,
        (normed, maps, w_own, w_other),
        (pltpu.VMEM, pltpu.VMEM, pl.ANY, pl.ANY),
        [
            (shape, BF)
            for shape in ((slots, width), (slots, width), (2, slots, columns), (heads, slots, slots))
        ],
        [
            pltpu.VMEM((2, *w_own.shape), BF),
            pltpu.VMEM((slots, width), BF),
            pltpu.VMEM((8, slots), F32),
            pltpu.SemaphoreType.DMA((2,)),
        ],
    )


def back(
    context_grad, maps, buffer, attended_grad, gathered, hidden_t, ct_t,
    mask, x, mixed_grad, logit_grad, layer_own, second_sums, gain, shift, router, place, want,
    act, pre_grad, w_own, w_other, proj, probs, capacity, orders,
):
    slots, width = buffer.shape
    columns = proj.shape[2]
    hidden = act.shape[2]
    loaded = (buffer, attended_grad, gathered, hidden_t, ct_t, x, mixed_grad, layer_own)
    count = x.shape[0]
    peers = lax.axis_size("dp")
    vmem, hbm = pltpu.VMEM, pl.ANY
    dma = pltpu.SemaphoreType.DMA
    rows = width // peers
    after = []
    if orders is None:
        outs = [((width, hidden), BF)] * 3
    else:
        outs = [((rows, hidden), F32)] * 3
        counts = [peers >> (stage + 1) for stage in range(len(orders[0]))]
        for size in (hidden, hidden, hidden // 2, hidden // 2):
            after += [dma((sum(counts),))] * 2
            after += [vmem((n, rows, size), BF) for n in counts]
    outs += [((place.shape[0], width), BF), ((place.shape[0], width), F32), ((8, width), F32)]
    chunks = 2 * (hidden // (512 if hidden % 512 == 0 else hidden)) + 4
    wide = vmem((width, hidden), BF)
    sums_stages = peers.bit_length()
    return exchange_call(
        lambda whole, *refs: back_kernel(whole, orders, *refs), "back", 1, capacity,
        (context_grad, maps, mask, logit_grad, second_sums, gain, shift, router, place, want,
         act, pre_grad, w_own, w_other, proj, probs, *loaded),
        (vmem,) * 10 + (hbm,) * (6 + len(loaded)),
        outs,
        [
            vmem((2 * count, hidden), BF), vmem((2 * count, hidden), BF),
            vmem((2, *w_own.shape), BF), vmem(proj.shape, BF), vmem(probs.shape, BF),
            vmem((slots, width), BF), vmem((2, slots, columns), BF), vmem((slots, width), BF),
            wide, wide, wide, wide,
            *((wide, wide) if orders else [vmem((16, 128), BF)] * 2),
            vmem((sums_stages, 8, width), F32), vmem((sums_stages, 8, width), F32),
            vmem((2, 128, width), BF), vmem((2, 128, width), F32), dma((2, 2)),
            *[vmem(value.shape, value.dtype) for value in loaded],
            dma((8 + len(loaded),)), dma((chunks,)), dma((chunks,)), dma((sums_stages,)), dma((sums_stages,)),
            pltpu.SemaphoreType.REGULAR,
        ],
        after,
        (vmem, vmem, vmem, hbm, hbm, vmem),
    )


def half_erfc(value, bell):
    t = 1.0 / (1.0 + (0.3275911 * 0.5**0.5) * jnp.abs(value))
    poly = 1.061405429 * t - 1.453152027
    poly = poly * t + 1.421413741
    poly = poly * t - 0.284496736
    poly = poly * t + 0.254829592
    return 0.5 * poly * t * bell


def row_sums(value):
    return jnp.sum(value.reshape(value.shape[0] // 8, 8, value.shape[1]), axis=0)


def feed_kernel(
    gathered, mask, x, ct, gate, gain, shift, wo_own, wo_other, we_own, we_other, wr_own, wr_other,
    layer, mixed_grad, attended_grad, context_grad, logit_grad, sums, hidden_t, ct_t, act_out, pre_out,
    we, wr, attended, mixed, nhat, inv, hidden, mlp, hidden_grad, pre, act_grad, act, pre_grad,
    we_sem, wr_sem, act_sem, pre_sem,
):
    core = lax.axis_index("mp")
    slots, width = gathered.shape
    count = x.shape[0]
    columns = we_own.shape[1]
    chunk = pre.shape[1]
    steps = columns // chunk
    cols = wo_own.shape[0]
    step_rows = 32

    def chunk_loads(i, j):
        at = pl.ds(pl.multiple_of(j * chunk, 128), chunk)
        here_e, here_r = (we_own, wr_own) if i == 0 else (we_other, wr_other)
        return (
            pltpu.make_async_copy(here_e.at[:, at], we.at[i * steps + j], we_sem.at[i * steps + j]),
            pltpu.make_async_copy(here_r.at[at, :], wr.at[i * steps + j], wr_sem.at[i * steps + j]),
        )

    for i in range(2):
        for j in range(steps):
            for load in chunk_loads(i, j):
                load.start()

    own_cols = pl.ds(pl.multiple_of(core * cols, 128), cols)
    other_cols = pl.ds(pl.multiple_of((1 - core) * cols, 128), cols)
    attended[...] = mm(gathered[:, own_cols], wo_own[...], ((1,), (0,))) + mm(
        gathered[:, other_cols], wo_other[...], ((1,), (0,))
    )

    def rows_of(r):
        return pl.ds(pl.multiple_of(r * step_rows, step_rows), step_rows)

    def norm_rows(r, carry, kept):
        at = rows_of(r)
        value = x[at, :].astype(F32)
        if kept:
            shown = jnp.where(mask[at, :] > 0.5, attended[at, :], 0.0)
            attended[at, :] = shown
            value = value + gate[at, :] * shown
        mixed[at, :] = value
        normal, scale = norm_stats(value)
        nhat[at, :] = normal
        inv[at, :] = scale
        hidden[at, :] = (normal * gain[...] + shift[...]).astype(BF)
        mlp[at, :] = jnp.zeros((step_rows, width), F32)
        hidden_grad[at, :] = jnp.zeros((step_rows, width), F32)
        return carry

    kept_steps = slots // step_rows
    lax.fori_loop(0, kept_steps, functools.partial(norm_rows, kept=True), 0)
    lax.fori_loop(kept_steps, count // step_rows, functools.partial(norm_rows, kept=False), 0)
    hidden_t[...] = hidden[...].T
    ct_t[...] = ct[...].T

    def outs(i, j):
        at = pl.ds(pl.multiple_of(j * chunk, 128), chunk)
        n = i * steps + j
        return (
            pltpu.make_async_copy(act.at[n % 2], act_out.at[i, :, at], act_sem.at[n]),
            pltpu.make_async_copy(pre_grad.at[n % 2], pre_out.at[i, :, at], pre_sem.at[n]),
        )

    for n, (i, j) in enumerate([(i, j) for i in range(2) for j in range(steps)]):
        for load in chunk_loads(i, j):
            load.wait()
        w_e, w_r = we[n], wr[n]
        pre[...] = mm(hidden[...], w_e, ((1,), (0,)))
        act_grad[...] = mm(ct[...], w_r, ((1,), (1,)))
        if n >= 2:
            m = n - 2
            for out in outs(m // steps, m % steps):
                out.wait()

        def gelu_rows(r, carry, n=n):
            at = pl.ds(pl.multiple_of(r * 16, 16), 16)
            value = pre[at, :]
            bell = jnp.exp(-0.5 * value * value)
            tail = half_erfc(value, bell)
            phi = jnp.where(value < 0.0, tail, 1.0 - tail)
            act[n % 2, at, :] = (value * phi).astype(BF)
            slope = phi + value * bell * 0.3989422804014327
            pre_grad[n % 2, at, :] = (act_grad[at, :] * slope).astype(BF)
            return carry

        lax.fori_loop(0, count // 16, gelu_rows, 0, unroll=2)
        for out in outs(i, j):
            out.start()
        mlp[...] += mm(act[n % 2], w_r, ((1,), (0,)))
        hidden_grad[...] += mm(pre_grad[n % 2], w_e, ((1,), (1,)))

    def back_rows(r, carry, kept):
        at = rows_of(r)
        layer[at, :] = (mixed[at, :] + mlp[at, :]).astype(BF)
        grad = hidden_grad[at, :]
        normal = nhat[at, :]
        total = ct[at, :].astype(F32) + norm_pull(grad * gain[...], normal, inv[at, :])
        mixed_grad[at, :] = total
        if kept:
            scale = gate[at, :]
            attended_grad[at, :] = jnp.where(mask[at, :] > 0.5, scale * total, 0.0).astype(BF)
            logit_grad[at, :] = (
                jnp.sum(total * attended[at, :], axis=-1, keepdims=True) * scale * (1.0 - scale)
            )
        else:
            logit_grad[at, :] = jnp.zeros((step_rows, 1), F32)
        return (carry[0] + row_sums(grad * normal), carry[1] + row_sums(grad))

    zeros = jnp.zeros((8, width), F32)
    carry = lax.fori_loop(0, kept_steps, functools.partial(back_rows, kept=True), (zeros, zeros))
    carry = lax.fori_loop(
        kept_steps, count // step_rows, functools.partial(back_rows, kept=False), carry
    )
    for i in range(2):
        sums[i : i + 1, :] = jnp.sum(carry[i], axis=0, keepdims=True)
    for w, at in ((wo_own, own_cols), (wo_other, other_cols)):
        part = mm(attended_grad[...], w[...], ((1,), (1,)))
        context_grad[:, at] = jnp.where(mask[...] > 0.5, part, 0.0).astype(BF)
    last = 2 * steps
    for n in range(max(0, last - 2), last):
        for out in outs(n // steps, n % steps):
            out.wait()


def feed(gathered, mask, x, ct, gate, gain, shift, w_output_2, w_expand_2, w_reduce_2):
    slots, width = gathered.shape
    count = x.shape[0]
    columns = w_expand_2[0].shape[1]
    chunk = 512 if columns % 512 == 0 else columns
    steps = columns // chunk
    vmem, hbm = pltpu.VMEM, pl.ANY
    dma = pltpu.SemaphoreType.DMA
    outs = [
        ((count, width), BF, vmem), ((count, width), F32, vmem), ((slots, width), BF, vmem),
        ((slots, width), BF, vmem), ((count, 1), F32, vmem), ((2, width), F32, vmem),
        ((width, count), BF, vmem), ((width, count), BF, vmem),
        ((2, count, columns), BF, hbm), ((2, count, columns), BF, hbm),
    ]
    return pl.pallas_call(
        feed_kernel,
        out_shape=[jax.ShapeDtypeStruct(shape, kind) for shape, kind, _ in outs],
        in_specs=[pl.BlockSpec(memory_space=space) for space in (vmem,) * 9 + (hbm,) * 4],
        out_specs=[pl.BlockSpec(memory_space=space) for _, _, space in outs],
        scratch_shapes=[
            vmem((2 * steps, width, chunk), BF), vmem((2 * steps, chunk, width), BF),
            vmem((slots, width), F32), vmem((count, width), F32), vmem((count, width), F32),
            vmem((count, 1), F32), vmem((count, width), BF), vmem((count, width), F32),
            vmem((count, width), F32), vmem((count, chunk), F32), vmem((count, chunk), F32),
            vmem((2, count, chunk), BF), vmem((2, count, chunk), BF),
            *[dma((2 * steps,))] * 4,
        ],
        compiler_params=pltpu.CompilerParams(vmem_limit_bytes=48 * 2**20),
        name="feed",
    )(gathered, mask, x, ct, gate, gain[None], shift[None], *w_output_2, *w_expand_2, *w_reduce_2)


def shards(
    tokens,
    row_ids,
    select,
    priority,
    first_gain,
    first_shift,
    router,
    w_attend,
    w_output,
    second_gain,
    second_shift,
    w_expand,
    w_reduce,
    cotangent,
):
    dp_count = lax.axis_size("dp")
    mp_count = lax.axis_size("mp")
    core = lax.axis_index("mp")
    bits = dp_count.bit_length() - 1
    order_a = list(range(bits))
    order_b = [1, 0] + list(range(bits - 1, 1, -1))
    rows = dp_count * mp_count
    capacity = 5 * ROW_LEN // (8 * dp_count)
    count, width = tokens.shape
    own = count // mp_count
    own_pad = -(-own // 128) * 128
    slots = dp_count * capacity
    heads_cols = w_attend.shape[2]
    whole, left, parts = block_plan(capacity, width)
    maps = rest_map(dp_count, left, parts)

    w_attend = w_attend.transpose(1, 0, 2)
    w_attend_2 = (w_attend, swap(w_attend))
    w_output_2 = (w_output, swap(w_output))
    w_expand_2 = (w_expand, swap(w_expand))
    w_reduce_2 = (w_reduce, swap(w_reduce))

    chosen = select == 1
    same_row = row_ids[:, None] == row_ids[None, :]
    earlier = priority[None, :] < priority[:, None]
    rank = jnp.sum((same_row & earlier & chosen[None, :]).astype(jnp.int32), axis=1)
    kept = chosen & (rank < capacity)
    taken = jnp.sum(
        ((row_ids[None, :] == jnp.arange(rows)[:, None]) & kept[None, :]).astype(jnp.int32), axis=1
    )
    at = jnp.arange(slots)
    row_at = jnp.where(at < dp_count * whole, at // max(whole, 1), (at - dp_count * whole) // left)
    rank_at = jnp.where(
        at < dp_count * whole, at % max(whole, 1), whole + (at - dp_count * whole) % left
    )
    hits = (row_at[:, None] == jnp.arange(dp_count)[None, :]).astype(jnp.int32)
    taken_at = jnp.sum(hits[None] * taken.reshape(dp_count, mp_count).T[:, None, :], axis=2)
    filled = rank_at[None, :] < taken_at
    filled_all = jnp.pad(filled, ((0, 0), (0, own - slots))).reshape(count)
    peer = row_ids // mp_count
    place = jnp.where(
        kept,
        (row_ids % mp_count) * own
        + jnp.where(
            rank < whole, peer * whole + rank, dp_count * whole + peer * left + rank - whole
        ),
        count + jnp.cumsum(jnp.where(kept, 0, 1)),
    )
    want = jnp.where(filled_all, jnp.arange(count), count + jnp.cumsum(jnp.where(filled_all, 0, 1)))
    want = jnp.pad(want.reshape(mp_count, own), ((0, 0), (0, own_pad - own)), constant_values=-1)
    want_own = jnp.where(core == 0, want[0], want[1])
    want_other = jnp.where(core == 0, want[1], want[0])
    mask = jnp.where(core == 0, filled[0], filled[1])[:, None]
    pick_own = (want_own[:, None] == place[None, :]).astype(BF)

    x = mm(pick_own, tokens, ((1,), (0,)))
    ct = mm(pick_own, cotangent, ((1,), (0,))).astype(BF)

    nhat_1, inv_1 = norm_stats(x)
    normed = (nhat_1 * first_gain + first_shift).astype(BF)
    normed_wide = normed.astype(F32)
    mask_wide, x_low = mask.astype(F32), x.astype(BF)
    gate = jax.nn.sigmoid(jnp.sum(normed_wide * router, axis=-1, keepdims=True))

    gathered, buffer, proj, probs = attend(
        jnp.where(mask, normed[:slots], jnp.asarray(EMPTY, BF)), maps, *w_attend_2, capacity
    )
    (layer_own, mixed_grad, attended_grad, context_grad, logit_grad, sums, hidden_t, ct_t, acts, pre_grads) = feed(
        gathered, mask_wide, x_low, ct, gate, second_gain, second_shift,
        w_output_2, w_expand_2, w_reduce_2,
    )
    place_pad = jnp.pad(place.astype(jnp.int32), (0, -count % 16), constant_values=-2)[:, None]
    orders = (order_a, order_b) if width // dp_count % 16 == 0 else None
    expand_sum, reduce_sum, late_sum, layer_out, tokens_grad, vectors = back(
        context_grad, maps, buffer, attended_grad, gathered, hidden_t, ct_t,
        mask_wide, x_low, mixed_grad, logit_grad, layer_own, sums, first_gain[None], first_shift[None],
        router[None], place_pad, jnp.concatenate([want_own, want_other])[None].astype(jnp.int32),
        acts, pre_grads, *w_attend_2, proj, probs, capacity, orders,
    )
    if orders is None:
        expand_sum = scatter_sum(expand_sum, order_a)
        reduce_sum = scatter_sum(reduce_sum, order_b)
        late_sum = scatter_sum(late_sum, order_a)
    rows_here = width // dp_count
    vectors = lax.dynamic_slice_in_dim(vectors, lax.axis_index("dp") * rows_here, rows_here, 1)

    attend_cols = 3 * heads_cols
    return (
        layer_out[:count],
        tokens_grad[:count],
        vectors[0],
        vectors[1],
        vectors[2],
        late_sum[:, :attend_cols].reshape(-1, 3, heads_cols),
        late_sum[:, attend_cols:].T,
        vectors[3],
        vectors[4],
        expand_sum,
        reduce_sum.T,
    )


def solution(mesh):
    in_specs = (
        P("dp", None),
        P("dp"),
        P("dp"),
        P("dp"),
        P(),
        P(),
        P(),
        P(None, None, "mp"),
        P("mp", None),
        P(),
        P(),
        P(None, "mp"),
        P("mp", None),
        P("dp", None),
    )
    out_specs = (
        P("dp", None),
        P("dp", None),
        P("dp"),
        P("dp"),
        P("dp"),
        P("dp", None, "mp"),
        P("mp", "dp"),
        P("dp"),
        P("dp"),
        P("dp", "mp"),
        P("mp", "dp"),
    )
    return jax.shard_map(shards, mesh=mesh, in_specs=in_specs, out_specs=out_specs, check_vma=False)
```

profile of v0, /device:TPU:0, one launch (start us, length us, event | category | flops | bytes accessed | tf_op | source)
XLA Modules:
  0.0 245.5 jit_solution(6335676195710972553)
XLA Ops:
  0.7 0.5 collective-permute-start
  1.3 0.4 collective-permute-start.3
  1.8 0.7 broadcast_compare_fusion.1
  2.5 2.7 %convert_reduce_fusion = s32[1154]{0:T(1024)S(1)} fusion(s32[1154]{0:T(1024)} %param.17, s32[1154]{0:T(1024)} %param.15, pred[1154]{0:T(1024)(128)(4,1)S(1)} %broadcast_compare_fusion.1), kind=kLoop, calls=%fused_computation | loop fusion | flops 7989142 | bytes 15002 | tf_op jit(solution)/shard_map/reduce_sum | solution.py:971
  5.2 0.7 broadcast_select_fusion.2
  5.9 0.8 convert_reduce_fusion.1
  6.7 0.1 reshape.381
  6.8 0.1 copy.33
  6.9 0.1 multiply_reduce_fusion.2
  7.1 0.3 reduce-window.16
  7.5 0.1 slice_reduce_fusion.1
  7.8 0.3 reduce-window.24
  8.2 0.1 slice_reduce_fusion
  8.4 0.7 fusion.15
  9.2 1.6 fusion.44
  10.8 0.4 multiply_reduce_fusion.1
  11.2 0.3 copy-done.13
  11.5 1.9 multiply_reduce_fusion
  13.4 0.6 broadcast_in_dim.42.refs_5_
  14.0 0.6 broadcast_in_dim.43.refs_6_
  14.6 0.6 broadcast_in_dim.76.refs_7_
  15.2 0.1 div.73.gate
  15.3 0.1 copy.34.mask.refs_2_
  15.5 0.6 broadcast_in_dim.78.refs_9_
  16.1 1.1 broadcast_in_dim.79.refs_8_
  17.4 0.1 broadcast_compare_fusion
  17.5 2.0 slice_select_fusion.normed
  19.4 0.8 and_convert_fusion.maps.refs_1_
  20.2 3.9 %fusion.8.ct = bf16[640,768]{1,0:T(8,128)(2,1)} fusion(bf16[1154,768]{1,0:T(8,128)(2,1)} %param.27, s32[1154]{0:T(1024)S(1)} %fusion.15, s32[640]{0:T(1024)S(1)} %get-tuple-element.85), kind=kOutput, calls=%fused_computation.12 | convolution fusion | flops 1135658240 | bytes 2762760 | tf_op jit(solution)/shard_map/dot_general | solution.py:22
  24.1 40.7 %attend.1 = (bf16[352,768]{1,0:T(8,128)(2,1)}, bf16[352,768]{1,0:T(8,128)(2,1)}, bf16[2,352,1152]{2,1,0:T(8,128)(2,1)}, bf16[12,352,352]{2,1,0:T(8,128)(2,1)}) custom-call(bf16[352,768]{1,0:T(8,128)(2,1)} %slice_select_fusion.normed, bf16[2,256,96]{2,1,0:T(8,128)(2,1)} %and_convert_fusion.maps.refs_1_, bf16[3,768,384]{2,1,0:T(8,128)(2,1)} %bitcast.32, ...), custom_call_target="tpu_custom_call" | custom-call | tf_op jit(solution)/shard_map/attend/pallas_call | solution.py:666
  65.0 1.0 copy-done.1
  66.0 49.3 %feed.1 = (bf16[640,768]{1,0:T(8,128)(2,1)S(1)}, f32[640,768]{1,0:T(8,128)}, bf16[352,768]{1,0:T(8,128)(2,1)S(1)}, bf16[352,768]{1,0:T(8,128)(2,1)S(1)}, f32[640...) custom-call(bf16[352,768]{1,0:T(8,128)(2,1)S(1)} %copy-done.1, ...), custom_call_target="tpu_custom_call" | custom-call | tf_op jit(solution)/shard_map/feed/pallas_call | solution.py:912
  115.4 0.9 copy-done.3
  116.3 0.9 copy-done.4
  117.2 0.9 copy-done.6
  118.1 0.8 copy-done.7
  118.9 0.8 copy-done.8
  119.7 0.6 copy-done.9
  120.3 113.6 %back.1 = (f32[48,1536]{1,0:T(8,128)}, f32[48,1536]{1,0:T(8,128)}, f32[48,1536]{1,0:T(8,128)}, bf16[1168,768]{1,0:T(8,128)(2,1)}, f32[1168,768]{1,0:T(8,128)}, /*index=5*/f32[8,768]{1,0:T(8,128)}) custom-call(bf16[352,768]{1,0:T(8,128)(2,1)} %copy-done.7, bf16[2,256,96]{2,1,0:T(8,128)(2,1)} %and_convert_fusion.maps.refs_1_, f32[352,1]{1,0:T(8,128)} %copy-done.2, ...), custom_call_target="tpu_custom_call" | custom-call | tf_op jit(solution)/shard_map/back/pallas_call | solution.py:666
  233.9 1.0 slice.80
  234.8 1.5 slice_bitcast_fusion
  236.4 4.2 %slice.76 = f32[1154,768]{1,0:T(8,128)} slice(f32[1168,768]{1,0:T(8,128)} %get-tuple-element.46), slice={[0:1154], [0:768]} | slice | bytes 7090176 | tf_op jit(solution)/shard_map/slice | solution.py:1035
  240.5 1.3 slice.75
  241.9 0.7 copy.41
  242.6 0.8 constant_dynamic-slice_fusion
  243.3 0.5 slice_bitcast_fusion.1
  243.9 0.7 copy.44
  244.6 0.7 copy.45
  (67 shorter events, 1.1 us)
Async XLA Ops:
  0.6 8.5 %copy-start = (bf16[1154,768]{1,0:T(8,128)(2,1)S(1)}, bf16[1154,768]{1,0:T(8,128)(2,1)}, u32[]{:S(2)}) copy-start(bf16[1154,768]{1,0:T(8,128)(2,1)} %param.14) | copy-start | bytes 5317636
  0.7 23.5 %collective-permute-start = (bf16[3,768,384]{2,1,0:T(8,128)(2,1)}, bf16[3,768,384]{2,1,0:T(8,128)(2,1)}, u32[]{:S(2)}, u32[]{:S(2)}) collective-permute-start(bf16[3,768,384]{2,1,0:T(8,128)(2,1)} %bitcast.31), channel_id=1, source_target_pairs={{0,1},{1,0},{2,3},{3,2},{4,5},{5,4},{6,7},{7,6},{8,9},{9,8},{10,11... | collective-permute-start | bytes 5308424 | tf_op jit(solution)/shard_map/ppermute | solution.py:36
  1.2 63.7 %collective-permute-start.2 = (bf16[768,1536]{1,0:T(8,128)(2,1)}, bf16[768,1536]{1,0:T(8,128)(2,1)}, u32[]{:S(2)}, u32[]{:S(2)}) collective-permute-start(bf16[768,1536]{1,0:T(8,128)(2,1)} %we_own.1), channel_id=1, source_target_pairs={{0,1},{1,0},{2,3},{3,2},{4,5},{5,4},{6,7},{7,6},{8,9},{9,8},{10,11... | collective-permute-start | bytes 7077896 | tf_op jit(solution)/shard_map/ppermute | solution.py:36
  1.3 63.7 %collective-permute-start.3 = (bf16[1536,768]{1,0:T(8,128)(2,1)}, bf16[1536,768]{1,0:T(8,128)(2,1)}, u32[]{:S(2)}, u32[]{:S(2)}) collective-permute-start(bf16[1536,768]{1,0:T(8,128)(2,1)} %wr_own.1), channel_id=1, source_target_pairs={{0,1},{1,0},{2,3},{3,2},{4,5},{5,4},{6,7},{7,6},{8,9},{9,8},{10,11... | collective-permute-start | bytes 7077896 | tf_op jit(solution)/shard_map/ppermute | solution.py:36
  1.7 63.2 %collective-permute-start.1 = (bf16[384,768]{1,0:T(8,128)(2,1)}, bf16[384,768]{1,0:T(8,128)(2,1)S(1)}, u32[]{:S(2)}, u32[]{:S(2)}) collective-permute-start(bf16[384,768]{1,0:T(8,128)(2,1)} %wo_own.1), channel_id=1, source_target_pairs={{0,1},{1,0},{2,3},{3,2},{4,5},{5,4},{6,7},{7,6},{8,9},{9,8},{10,11... | collective-permute-start | bytes 1769480 | tf_op jit(solution)/shard_map/ppermute | solution.py:36
  10.7 0.7 copy-start.13
  10.7 0.7 copy-start.14
  10.8 0.7 copy-start.15
  11.5 4.0 %copy-start.16 = (f32[768]{0:T(1024)S(1)}, f32[768]{0:T(1024)}, u32[]{:S(2)}) copy-start(f32[768]{0:T(1024)} %param.23) | copy-start | bytes 9220
  11.5 4.1 %copy-start.17 = (f32[768]{0:T(1024)S(1)}, f32[768]{0:T(1024)}, u32[]{:S(2)}) copy-start(f32[768]{0:T(1024)} %param.24) | copy-start | bytes 9220
  15.5 49.4 %copy-start.2 = (f32[352,1]{1,0:T(8,128)}, f32[352,1]{1,0:T(8,128)S(1)}, u32[]{:S(2)}) copy-start(f32[352,1]{1,0:T(8,128)S(1)} %copy.34.mask.refs_2_) | copy-start | bytes 4228
  24.1 40.8 %copy-start.5 = (bf16[384,768]{1,0:T(8,128)(2,1)S(1)}, bf16[384,768]{1,0:T(8,128)(2,1)}, u32[]{:S(2)}) copy-start(bf16[384,768]{1,0:T(8,128)(2,1)} %wo_own.1) | copy-start | bytes 1769476
  64.9 1.0 copy-start.1
  115.3 0.9 copy-start.3
  116.3 0.9 copy-start.4
  117.2 0.9 copy-start.6
  118.1 0.8 copy-start.7
  118.9 0.8 copy-start.8
  119.7 0.6 copy-start.9
  236.3 4.2 %copy-start.10 = (bf16[1168,768]{1,0:T(8,128)(2,1)S(1)}, bf16[1168,768]{1,0:T(8,128)(2,1)}, u32[]{:S(2)}) copy-start(bf16[1168,768]{1,0:T(8,128)(2,1)} %get-tuple-element.45) | copy-start | bytes 5382148
  240.5 3.3 %copy-start.12 = (f32[48,1536]{1,0:T(8,128)S(1)}, f32[48,1536]{1,0:T(8,128)}, u32[]{:S(2)}) copy-start(f32[48,1536]{1,0:T(8,128)} %get-tuple-element.120) | copy-start | bytes 884740
  240.5 4.0 %copy-start.11 = (f32[48,1536]{1,0:T(8,128)S(1)}, f32[48,1536]{1,0:T(8,128)}, u32[]{:S(2)}) copy-start(f32[48,1536]{1,0:T(8,128)} %get-tuple-element.50) | copy-start | bytes 884740
where the time goes:
time: 250 us; the launch traced here: 245 us
  Pallas kernels  204 us (82%)
  local copies, waits for them, and re-layouts  22.1 us (9%)
  other arithmetic  11.9 us (5%)
  matrix products  5.52 us (2%)
    pallas_call x2, Pallas kernels, exchange_call(): pl.pallas_call(functools.partial(kernel, whole), out_shape=[jax.ShapeDtyp...  154 us
    pallas_call x1, Pallas kernels, feed(): pl.pallas_call(feed_kernel, out_shape=[jax.ShapeDtypeStruct(shape, kind)...  49.3 us
    unnamed x38, local copies, waits for them, and re-layouts  7.71 us
    dot_general x2, matrix products, mm(): return lax.dot_general(a, b, (dims, ((), ())), preferred_element_type=F32)  5.52 us
  transfers between devices with their start and end apart: 4, of which 0 were waited for; matrix products, arithmetic and copies ran while one was open for 9% of the time, Pallas kernels for 17%

commit v1 on v0

v1 whole, which is shorter than its diff:
```python
import functools

import jax
import jax.numpy as jnp
import numpy as np
from jax import lax
from jax.experimental import pallas as pl
from jax.experimental.pallas import tpu as pltpu
from jax.sharding import PartitionSpec as P

HD = 64
ROW_LEN = 577
EPSILON = 1e-06
MASKED_SCORE = -1000000000.0
EMPTY = 1e30
BF = jnp.bfloat16
F32 = jnp.float32
MESH = pl.DeviceIdType.MESH


def mm(a, b, dims):
    return lax.dot_general(a, b, (dims, ((), ())), preferred_element_type=F32)


def norm_stats(value):
    center = value - jnp.mean(value, axis=-1, keepdims=True)
    inv = lax.rsqrt(jnp.mean(center * center, axis=-1, keepdims=True) + EPSILON)
    return center * inv, inv


def norm_pull(e, nhat, inv):
    return (e - jnp.mean(e, axis=-1, keepdims=True) - nhat * jnp.mean(e * nhat, axis=-1, keepdims=True)) * inv


def swap(value):
    return lax.ppermute(value, "mp", [(0, 1), (1, 0)])


def scatter_sum(grad, order):
    count = lax.axis_size("dp")
    me = lax.axis_index("dp")
    bits = count.bit_length() - 1
    width = grad.shape[0] // count
    dims = [2] * bits
    value = grad.reshape(dims + [width, grad.shape[1]])
    out = None
    for step in order:
        axis = bits - 1 - step
        mine = (me >> step) & 1
        give = lax.dynamic_slice_in_dim(value, 1 - mine, 1, axis)
        keep = lax.dynamic_slice_in_dim(value, mine, 1, axis)
        got = lax.ppermute(give, "dp", [(i, i ^ (1 << step)) for i in range(count)])
        out = keep.astype(F32) + got.astype(F32)
        value = out.astype(grad.dtype)
    return out.reshape(width, grad.shape[1])


def block_plan(capacity, width):
    whole = capacity // 16 * 16
    left = capacity - whole
    parts = max(s for s in (1, 2, 3, 6) if left * s <= 16 and width % (128 * s) == 0)
    return whole, left, parts


def rest_map(peers, left, parts):
    at = jnp.arange(peers * 16)[None, :, None]
    row = jnp.arange(peers * left)[None, None, :]
    part = jnp.arange(parts)[:, None, None]
    return ((at // 16 == row // left) & (at % 16 == part * left + row % left)).astype(BF)


def greet(peers, with_pair=False):
    me, core = lax.axis_index("dp"), lax.axis_index("mp")
    barrier = pltpu.get_barrier_semaphore()

    def hello(d, carry):
        pl.semaphore_signal(
            barrier, inc=1, device_id=(lax.rem(me + d, peers), core), device_id_type=MESH
        )
        return carry

    lax.fori_loop(1, peers, hello, 0)
    if with_pair:
        pl.semaphore_signal(barrier, inc=1, device_id=(me, 1 - core), device_id_type=MESH)
    return lambda: pl.semaphore_wait(barrier, peers if with_pair else peers - 1)


def pack(value, blocks, maps, whole):
    rest = blocks[-1]
    peers, lanes = rest.shape[0], rest.shape[2]
    if whole:
        blocks[0][...] = value[: peers * whole].reshape(peers, whole, value.shape[1])
    tail = value[peers * whole :]
    total = sum(
        mm(maps[i], tail[:, i * lanes : (i + 1) * lanes], ((1,), (0,)))
        for i in range(maps.shape[0])
    )
    rest[...] = total.astype(BF).reshape(peers, 16, lanes)


def unpack(blocks, maps, whole, out):
    rest = blocks[-1]
    peers, lanes = rest.shape[0], rest.shape[2]
    if whole:
        out[: peers * whole, :] = blocks[0][...].reshape(peers * whole, out.shape[1])
    left = rest[...].reshape(peers * 16, lanes)
    for i in range(maps.shape[0]):
        out[peers * whole :, i * lanes : (i + 1) * lanes] = mm(
            maps[i], left, ((0,), (0,))
        ).astype(BF)


def copies(d, pairs, sends, recvs, back=False):
    me, core = lax.axis_index("dp"), lax.axis_index("mp")
    peers = pairs[0][0].shape[0]
    to, source = lax.rem(me + d, peers), lax.rem(me + peers - d, peers)
    return [
        pltpu.make_async_remote_copy(
            src_ref=here.at[to],
            dst_ref=there.at[source if back else me],
            send_sem=sends.at[i, d],
            recv_sem=recvs.at[i, d],
            device_id=(to, core),
            device_id_type=MESH,
        )
        for i, (here, there) in enumerate(pairs)
    ]


def send_all(pairs, sends, recvs):
    me = lax.axis_index("dp")

    def start(d, carry):
        for copy in copies(d, pairs, sends, recvs):
            copy.start()
        return carry

    lax.fori_loop(1, pairs[0][0].shape[0], start, 0)
    for here, there in pairs:
        there[pl.ds(me, 1)] = here[pl.ds(me, 1)]


def wait_all(pairs, sends, recvs):
    def finish(d, carry):
        for copy in copies(d, pairs, sends, recvs, back=True):
            copy.wait_recv()
        return carry

    def drain(d, carry):
        for copy in copies(d, pairs, sends, recvs):
            copy.wait_send()
        return carry

    lax.fori_loop(1, pairs[0][0].shape[0], finish, 0)
    lax.fori_loop(1, pairs[0][0].shape[0], drain, 0)


def lane_masks():
    low = lax.broadcasted_iota(jnp.int32, (1, 128), 1) < HD
    return low, jnp.logical_not(low)


def routing(info, layout, capacity, count, wide_cols, hit_rows, routes, route_cols):
    core = lax.axis_index("mp").astype(F32)
    cores = lax.axis_size("mp")
    total = info.shape[1]
    blocks = total // 128
    row, chosen, priority = (info[i : i + 1, :].astype(F32) for i in range(3))
    device, slot, spot, side = (layout[i : i + 1, :].astype(F32) for i in range(4))
    core_of = core + side * (1.0 - 2.0 * core)
    row_of = device * cores + core_of
    spot_of = jnp.where(spot >= 0.0, core_of * total + spot, -1.0)
    low = row * 2048.0
    key = low + priority
    picked = chosen > 0.5
    hit_rows[...] = jnp.zeros(hit_rows.shape, F32)
    hit_rows[0:1, :] = jnp.where(picked, key, -1.0)
    hit_rows[1:2, :] = jnp.where(picked, row, -1.0)
    wide_cols[...] = hit_rows[...].T

    def fold(hit):
        return jnp.sum(jnp.where(hit, 1.0, 0.0).reshape(16, 8, total), axis=0)

    def count_rows(b, carry):
        at = pl.ds(pl.multiple_of(b * 128, 128), 128)
        keys, rows = wide_cols[at, 0:1], wide_cols[at, 1:2]
        return (
            carry[0] + fold((keys >= low) & (keys < key)),
            carry[1] + fold(rows == row_of),
        )

    zeros = jnp.zeros((8, total), F32)
    ranks, sizes = lax.fori_loop(0, blocks, count_rows, (zeros, zeros))
    rank = jnp.sum(ranks, axis=0, keepdims=True)
    size = jnp.sum(sizes, axis=0, keepdims=True)
    kept = picked & (rank < capacity)
    filled = slot < jnp.minimum(size, float(capacity))
    index = lax.broadcasted_iota(jnp.int32, (1, total), 1).astype(F32)
    rest = (index < count) & jnp.logical_not(kept)
    free = (spot_of >= 0.0) & jnp.logical_not(filled)
    hit_rows[0:1, :] = jnp.where(rest, index, 1e9)
    hit_rows[1:2, :] = jnp.where(free, spot_of, 1e9)
    wide_cols[...] = hit_rows[...].T

    def count_rest(b, carry):
        at = pl.ds(pl.multiple_of(b * 128, 128), 128)
        return (
            carry[0] + fold(wide_cols[at, 0:1] < index),
            carry[1] + fold(wide_cols[at, 1:2] < spot_of),
        )

    before, ahead = lax.fori_loop(0, blocks, count_rest, (zeros, zeros))
    base = float(lax.axis_size("dp") * cores * capacity)
    before = base + jnp.sum(before, axis=0, keepdims=True)
    ahead = base + jnp.sum(ahead, axis=0, keepdims=True)
    routes[...] = jnp.zeros(routes.shape, F32)
    routes[0:1, :] = jnp.where(
        filled, row_of * capacity + slot, jnp.where(spot_of >= 0.0, ahead, -1.0)
    )
    routes[1:2, :] = jnp.where(filled, 1.0, 0.0)
    routes[2:3, :] = jnp.where(kept, row * capacity + rank, jnp.where(rest, before, -2.0))
    route_cols[...] = routes[...].T


def attend_kernel(
    whole, capacity, info, layout, vectors, maps, tokens_in, cotangent_in, w_own, w_other,
    gathered, buffer, proj, probs, x, ct, gate, routes, route_cols,
    tokens, cotangent, wide_cols, hit_rows,
    w_vmem, context, key_mask, w_sem, send_1, recv_1, send_2, recv_2, *blocks,
):
    core = lax.axis_index("mp")
    loads = [
        pltpu.make_async_copy(here, there, w_sem.at[i])
        for i, (here, there) in enumerate(
            (
                (tokens_in, tokens),
                (cotangent_in, cotangent),
                (w_own, w_vmem.at[0]),
                (w_other, w_vmem.at[1]),
            )
        )
    ]
    for load in loads:
        load.start()
    given_1, taken_1, given_2, taken_2 = split_blocks(blocks)
    ready = greet(given_1[-1].shape[0])
    count, width = tokens.shape
    slots = buffer.shape[0]
    total_rows = x.shape[0]
    routing(info, layout, capacity, count, wide_cols, hit_rows, routes, route_cols)
    loads[0].wait()

    def pick(r, source, out):
        at = pl.ds(pl.multiple_of(r * 128, 128), 128)
        hit = (route_cols[at, 0:1] == routes[2:3, :count]).astype(F32).astype(BF)
        out[at, :] = mm(hit, source[...], ((1,), (0,))).astype(BF)

    def norm_rows(r, carry, sent):
        at = pl.ds(pl.multiple_of(r * 32, 32), 32)
        normal, _ = norm_stats(x[at, :].astype(F32))
        normed = (normal * vectors[0:1, :] + vectors[1:2, :]).astype(BF)
        wide = normed.astype(F32)
        gate[at, :] = jax.nn.sigmoid(jnp.sum(wide * vectors[2:3, :], axis=-1, keepdims=True))
        if sent:
            context[at, :] = jnp.where(route_cols[at, 1:2] > 0.5, wide, EMPTY).astype(BF)
        return carry

    def picks(first, last, source, out):
        def body(r, carry):
            pick(r, source, out)
            return carry

        lax.fori_loop(first, last, body, 0)

    kept_blocks = -(-slots // 128)
    picks(0, kept_blocks, tokens, x)
    lax.fori_loop(0, slots // 32, functools.partial(norm_rows, sent=True), 0)
    pack(context[...], given_1, maps, whole)
    ready()
    first = list(zip(given_1, taken_1))
    send_all(first, send_1, recv_1)
    picks(kept_blocks, total_rows // 128, tokens, x)
    lax.fori_loop(slots // 32, total_rows // 32, functools.partial(norm_rows, sent=False), 0)
    loads[1].wait()
    picks(0, total_rows // 128, cotangent, ct)
    wait_all(first, send_1, recv_1)
    unpack(taken_1, maps, whole, buffer)
    lane = (lax.broadcasted_iota(jnp.int32, (8, 128), 1) == 0).astype(F32).astype(BF)
    key_mask[...] = jnp.where(
        mm(lane, buffer[:, :128], ((1,), (1,))) < 0.5 * EMPTY, 1.0, 0.0
    )
    received = buffer[...].astype(F32)
    buffer[...] = jnp.where(received[:, :1] < 0.5 * EMPTY, received, 0.0).astype(BF)
    cols = w_own.shape[2]
    pairs = cols // 128
    masks = lane_masks()
    zero = jnp.zeros((), BF)
    for i in range(2):
        loads[2 + i].wait()
        for which in range(3):
            proj[i, :, which * cols : (which + 1) * cols] = mm(
                buffer[...], w_vmem[i, which], ((1,), (0,))
            ).astype(BF)
        canonical = core if i == 0 else 1 - core

        def pair_step(p, carry, i=i, canonical=canonical):
            def part(which):
                return proj[i, :, pl.ds(pl.multiple_of(which * cols + p * 128, 128), 128)]

            q, k, v = part(0), part(1), part(2)
            total = 0.0
            for e, lanes in enumerate(masks):
                scores = mm(q, jnp.where(lanes, k, zero), ((1,), (1,))) * HD ** (-0.5)
                scores = jnp.where(key_mask[:1, :] > 0.5, scores, MASKED_SCORE)
                weights = jnp.exp(scores - jnp.max(scores, axis=-1, keepdims=True))
                low = (weights * (1.0 / jnp.sum(weights, axis=-1, keepdims=True))).astype(BF)
                probs[(i * pairs + p) * 2 + e] = low
                total = total + mm(low, jnp.where(lanes, v, zero), ((1,), (0,)))
            context[:, pl.ds(pl.multiple_of(canonical * cols + p * 128, 128), 128)] = total.astype(BF)
            return carry

        lax.fori_loop(0, pairs, pair_step, 0)
    pack(context[...], given_2, maps, whole)
    second = list(zip(given_2, taken_2))
    send_all(second, send_2, recv_2)
    wait_all(second, send_2, recv_2)
    unpack(taken_2, maps, whole, gathered)


class Halving:
    def __init__(self, source, bufs, sends, recvs, order, out, window):
        self.source, self.bufs, self.sends, self.recvs = source, bufs, sends, recvs
        self.order, self.out, self.window = order, out, window
        self.stages = len(order)
        self.rows = bufs[0].shape[1]
        self.counts = [buf.shape[0] for buf in bufs]
        self.first = [k for stage, k in halving_plan(self.stages) if stage == 0]

    def bit(self, stage):
        return lax.rem(lax.div(lax.axis_index("dp"), 1 << self.order[stage]), 2)

    def block(self, k, kept):
        index = 0
        for stage in range(self.stages):
            mine = self.bit(stage)
            if stage == 0:
                value = mine if kept else 1 - mine
            else:
                part = lax.rem(lax.div(k, self.counts[stage]), 2)
                value = (1 - mine) * (1 - part) + mine * part
            index = index + value * (1 << self.order[stage])
        return pl.ds(pl.multiple_of(index * self.rows, 16), self.rows)

    def copy(self, stage, k):
        me, core = lax.axis_index("dp"), lax.axis_index("mp")
        to = me + (1 - 2 * self.bit(stage)) * (1 << self.order[stage])
        at = sum(self.counts[:stage]) + k
        src = self.source.at[self.block(k, False), :] if stage == 0 else self.bufs[stage - 1].at[k]
        return pltpu.make_async_remote_copy(
            src_ref=src,
            dst_ref=self.bufs[stage].at[k],
            send_sem=self.sends.at[at],
            recv_sem=self.recvs.at[at],
            device_id=(to, core),
            device_id_type=MESH,
        )

    def begin(self):
        for k in self.first[: self.window]:
            self.copy(0, k).start()

    def step(self, stage, k):
        self.copy(stage, k).wait_recv()
        buf = self.bufs[stage]
        if stage == 0:
            own = self.source[self.block(k, True), :]
        else:
            own = self.bufs[stage - 1][pl.ds(self.counts[stage] + k, 1)][0]
        total = own.astype(F32) + buf[pl.ds(k, 1)][0].astype(F32)
        if stage == self.stages - 1:
            self.out[...] = total
            return
        buf[pl.ds(k, 1)] = total.astype(BF)[None]
        if k < self.counts[stage + 1]:
            self.copy(stage + 1, k).start()
        if stage == 0:
            ahead = self.first.index(k) + self.window
            if ahead < len(self.first):
                self.copy(0, self.first[ahead]).start()

    def drain(self):
        for stage, count in enumerate(self.counts):

            def finish(k, carry, stage=stage):
                self.copy(stage, k).wait_send()
                return carry

            lax.fori_loop(0, count, finish, 0)


def halving_plan(stages):
    counts = [1 << (stages - 1 - stage) for stage in range(stages)]
    times = {}
    for stage, count in enumerate(counts):
        for k in range(count):
            if stage == 0:
                bits = [(k >> i) & 1 for i in range(stages - 1)]
                times[stage, k] = 1 + sum(bit << (stages - 2 - i) for i, bit in enumerate(bits))
            else:
                times[stage, k] = 1.6 + max(times[stage - 1, k], times[stage - 1, count + k])
    return sorted(times, key=lambda key: (times[key], key))


def advance(chains, steps):
    for stage, k in steps:
        for chain in chains:
            chain.step(stage, k)


def half_erfc(value, bell):
    t = 1.0 / (1.0 + (0.3275911 * 0.5**0.5) * jnp.abs(value))
    poly = 1.061405429 * t - 1.453152027
    poly = poly * t + 1.421413741
    poly = poly * t - 0.284496736
    poly = poly * t + 0.254829592
    return 0.5 * poly * t * bell


def row_sums(value):
    return jnp.sum(value.reshape(value.shape[0] // 8, 8, value.shape[1]), axis=0)


def back_kernel(
    whole, orders, maps, gate, vectors, routes, route_cols,
    gathered_in, wo_own, wo_other, x_in, ct_in, we_own, we_other, wr_own, wr_other,
    w_own, w_other, proj_in, probs_in, buffer_in,
    expand_out, reduce_out, late_out, layer_out, tokens_out, sums_out,
    gathered, wo, x, ct, w_vmem, proj, probs, buffer,
    we, wr, attended, mean, inv, hidden, hidden_t, ct_t, mlp, mixed_grad, pre, act_grad, act, pre_grad,
    logit_grad, attended_grad, upstream, proj_grad, layer_own, tokens_got,
    expand_give, reduce_give, expand_got, reduce_got, sums, sums_got, layer_stage, tokens_stage,
    load_sem, we_sem, wr_sem, out_sem, pair_send, pair_recv, sums_send, sums_recv, free_sem,
    send_1, recv_1, send_2, recv_2, *rest,
):
    dp, core = lax.axis_index("dp"), lax.axis_index("mp")
    peers = lax.axis_size("dp")
    width, columns = expand_give.shape
    slots = buffer.shape[0]
    count = x.shape[0]
    chunk = pre.shape[1]
    steps = columns // chunk
    cols = w_own.shape[2]
    pairs = cols // 128
    attend_cols = 3 * cols
    half = columns // 2
    step_rows = 32
    kept_steps, all_steps = slots // step_rows, count // step_rows
    ready = greet(peers, with_pair=True)
    gain, shift, router, gain_2, shift_2 = (vectors.at[pl.ds(i, 1), :] for i in range(5))

    def chunk_loads(n):
        j, slot = n // 2, n % 2
        here_e, here_r = (we_other, wr_other) if n % 2 == 0 else (we_own, wr_own)
        part = pl.ds(j * chunk, chunk)
        return (
            pltpu.make_async_copy(here_e.at[:, part], we.at[slot], we_sem.at[slot]),
            pltpu.make_async_copy(here_r.at[part, :], wr.at[slot], wr_sem.at[slot]),
        )

    local = [
        (gathered_in, gathered),
        (wo_own, wo.at[0]),
        (wo_other, wo.at[1]),
        (x_in, x),
        (ct_in, ct),
        (proj_in, proj),
        (probs_in, probs),
        (w_own, w_vmem.at[0]),
        (w_other, w_vmem.at[1]),
        (buffer_in, buffer),
    ]
    loads = [
        pltpu.make_async_copy(here, there, load_sem.at[i]) for i, (here, there) in enumerate(local)
    ]
    for load in (*loads[:5], *chunk_loads(0), *loads[5:]):
        load.start()

    kinds = 2 if whole else 1
    given_1, taken_1, given_2, taken_2 = split_blocks(rest[: 4 * kinds])
    rest = rest[4 * kinds :]
    late_give, late_got = reduce_give, expand_give
    chains = []
    plan = []
    if orders is not None:
        stages = len(orders[0])
        plan = halving_plan(stages)
        parts_of = []
        for j in range(steps):
            part = pl.ds(j * chunk, chunk)
            parts_of.append((expand_got.at[:, part], expand_out.at[:, part], orders[0], 8))
            parts_of.append((reduce_got.at[:, part], reduce_out.at[:, part], orders[1], 8))
        for j in range(2):
            part = pl.ds(j * half, half)
            parts_of.append((late_got.at[:, part], late_out.at[:, part], orders[j], 4))
        for i, (source, out, order, window) in enumerate(parts_of):
            mine = rest[i * (stages + 2) : (i + 1) * (stages + 2)]
            chains.append(Halving(source, mine[2:], mine[0], mine[1], order, out, window))
    done = [0] * (steps + 1)

    def run(group, number):
        if chains:
            advance(chains[2 * group : 2 * group + 2], plan[done[group] : done[group] + number])
            done[group] += number

    def begin(group):
        for chain in chains[2 * group : 2 * group + 2]:
            chain.begin()

    def pair_copy(at, give, got):
        return pltpu.make_async_remote_copy(
            src_ref=give,
            dst_ref=got,
            send_sem=pair_send.at[at],
            recv_sem=pair_recv.at[at],
            device_id=(dp, 1 - core),
            device_id_type=MESH,
        )

    def weight_copy(i, j):
        give, got = ((expand_give, expand_got), (reduce_give, reduce_got))[i]
        part = pl.ds(j * chunk, chunk)
        return pair_copy(i * steps + j, give.at[:, part], got.at[:, part])

    own_cols = pl.ds(pl.multiple_of(core * cols, 128), cols)
    other_cols = pl.ds(pl.multiple_of((1 - core) * cols, 128), cols)
    for load in loads[:3]:
        load.wait()
    attended[...] = mm(gathered[:, own_cols], wo[0], ((1,), (0,))) + mm(
        gathered[:, other_cols], wo[1], ((1,), (0,))
    )
    for load in loads[3:5]:
        load.wait()

    def rows_of(r):
        return pl.ds(pl.multiple_of(r * step_rows, step_rows), step_rows)

    def mixed_rows(rows, kept):
        value = x[rows, :].astype(F32)
        return value + gate[rows, :] * attended[rows, :] if kept else value

    def norm_rows(r, carry, kept):
        rows = rows_of(r)
        if kept:
            attended[rows, :] = jnp.where(route_cols[rows, 1:2] > 0.5, attended[rows, :], 0.0)
        value = mixed_rows(rows, kept)
        middle = jnp.mean(value, axis=-1, keepdims=True)
        center = value - middle
        scale = lax.rsqrt(jnp.mean(center * center, axis=-1, keepdims=True) + EPSILON)
        mean[rows, :] = middle
        inv[rows, :] = scale
        hidden[rows, :] = (center * scale * gain_2[...] + shift_2[...]).astype(BF)
        mlp[rows, :] = jnp.zeros((step_rows, width), F32)
        mixed_grad[rows, :] = jnp.zeros((step_rows, width), F32)
        return carry

    lax.fori_loop(0, kept_steps, functools.partial(norm_rows, kept=True), 0)
    lax.fori_loop(kept_steps, all_steps, functools.partial(norm_rows, kept=False), 0)
    hidden_t[...] = hidden[...].T
    ct_t[...] = ct[...].T

    def gelu_rows(r, carry):
        rows = pl.ds(pl.multiple_of(r * 16, 16), 16)
        value = pre[rows, :]
        bell = jnp.exp(-0.5 * value * value)
        tail = half_erfc(value, bell)
        phi = jnp.where(value < 0.0, tail, 1.0 - tail)
        act[rows, :] = (value * phi).astype(BF)
        slope = phi + value * bell * 0.3989422804014327
        pre_grad[rows, :] = (act_grad[rows, :] * slope).astype(BF)
        return carry

    for n in range(2 * steps):
        j, slot, is_own = n // 2, n % 2, n % 2 == 1
        part = pl.ds(j * chunk, chunk)
        for load in chunk_loads(n):
            load.wait()
        if n + 1 < 2 * steps:
            for load in chunk_loads(n + 1):
                load.start()

        def point(n=n, j=j, is_own=is_own):
            for group in range(j):
                run(group, 1)

        pre[...] = mm(hidden[...], we[slot], ((1,), (0,)))
        act_grad[...] = mm(ct[...], wr[slot], ((1,), (1,)))
        point()
        lax.fori_loop(0, count // 16, gelu_rows, 0, unroll=2)
        point()
        mlp[...] += mm(act[...], wr[slot], ((1,), (0,)))
        mixed_grad[...] += mm(pre_grad[...], we[slot], ((1,), (1,)))
        point()
        for i, (left, right, give, got) in enumerate(
            (
                (hidden_t, pre_grad, expand_give, expand_got),
                (ct_t, act, reduce_give, reduce_got),
            )
        ):
            value = mm(left[...], right[...], ((1,), (0,)))
            if is_own:
                weight_copy(i, j).wait_recv()
                got[:, part] = (value + got[:, part].astype(F32)).astype(BF)
            else:
                give[:, part] = value.astype(BF)
                if n == 0 and i == 0:
                    ready()
                weight_copy(i, j).start()
        point()
        if is_own:
            begin(j)

    def back_rows(r, carry, kept):
        rows = rows_of(r)
        mixed = mixed_rows(rows, kept)
        layer_own[rows, :] = (mixed + mlp[rows, :]).astype(BF)
        grad = mixed_grad[rows, :]
        scale = inv[rows, :]
        normal = (mixed - mean[rows, :]) * scale
        total = ct[rows, :].astype(F32) + norm_pull(grad * gain_2[...], normal, scale)
        mixed_grad[rows, :] = total
        if kept:
            open_by = gate[rows, :]
            attended_grad[rows, :] = jnp.where(route_cols[rows, 1:2] > 0.5, open_by * total, 0.0).astype(BF)
            logit_grad[rows, :] = (
                jnp.sum(total * attended[rows, :], axis=-1, keepdims=True) * open_by * (1.0 - open_by)
            )
        else:
            logit_grad[rows, :] = jnp.zeros((step_rows, 1), F32)
        return (carry[0] + row_sums(grad * normal), carry[1] + row_sums(grad))

    zeros = jnp.zeros((8, width), F32)
    carry = lax.fori_loop(0, kept_steps, functools.partial(back_rows, kept=True), (zeros, zeros))
    for group in range(steps - 1):
        run(group, 2)
    for at, w in ((own_cols, wo[0]), (other_cols, wo[1])):
        upstream[:, at] = mm(attended_grad[...], w, ((1,), (1,))).astype(BF)
    pack(upstream[...], given_1, maps, whole)
    first = list(zip(given_1, taken_1))
    send_all(first, send_1, recv_1)
    carry = lax.fori_loop(kept_steps, all_steps, functools.partial(back_rows, kept=False), carry)
    for i in range(2):
        sums[0, 3 + i : 4 + i, :] = jnp.sum(carry[i], axis=0, keepdims=True)
    sums[0, 5:8, :] = jnp.zeros((3, width), F32)

    for i in range(2):
        for j in range(steps):
            weight_copy(i, j).wait_send()
    pl.semaphore_signal(free_sem, inc=1, device_id=(dp, 1 - core), device_id_type=MESH)
    late_give[:, attend_cols:] = mm(
        attended_grad[...], gathered[:, other_cols], ((0,), (0,))
    ).astype(BF)
    output_own = mm(attended_grad[...], gathered[:, own_cols], ((0,), (0,)))
    pl.semaphore_wait(free_sem, 1)
    layer_copy = pair_copy(2 * steps + 3, layer_own, ct)
    layer_copy.start()
    output_copy, attend_copy = (
        pair_copy(2 * steps + i, late_give.at[:, part], late_got.at[:, part])
        for i, part in enumerate(
            (pl.ds(attend_cols, columns - attend_cols), pl.ds(0, attend_cols))
        )
    )
    output_copy.start()
    output_copy.wait_recv()
    late_got[:, attend_cols:] = (output_own + late_got[:, attend_cols:].astype(F32)).astype(BF)
    for group in range(steps - 1):
        run(group, 15)
    run(steps - 1, 2)

    wait_all(first, send_1, recv_1)
    unpack(taken_1, maps, whole, upstream)
    for load in loads[5:]:
        load.wait()
    masks = lane_masks()
    zero = jnp.zeros((), BF)
    for i in range(2):
        canonical = core if i == 0 else 1 - core

        def pair_step(p, carry, i=i, canonical=canonical):
            def place_of(which):
                return pl.ds(pl.multiple_of(which * cols + p * 128, 128), 128)

            q, k, v = (proj[i, :, place_of(which)] for which in range(3))
            up = upstream[:, place_of(canonical)]
            q_grad = k_grad = v_grad = 0.0
            for e, lanes in enumerate(masks):
                low = probs[(i * pairs + p) * 2 + e]
                wide = low.astype(F32)
                probs_grad = mm(up, jnp.where(lanes, v, zero), ((1,), (1,)))
                delta = jnp.sum(wide * probs_grad, axis=-1, keepdims=True)
                scores_grad = (wide * (probs_grad - delta)).astype(BF)
                v_grad = v_grad + mm(low, jnp.where(lanes, up, zero), ((0,), (0,)))
                q_grad = q_grad + mm(scores_grad, jnp.where(lanes, k, zero), ((1,), (0,)))
                k_grad = k_grad + mm(scores_grad, jnp.where(lanes, q, zero), ((0,), (0,)))
            proj_grad[i, :, place_of(0)] = (q_grad * HD ** (-0.5)).astype(BF)
            proj_grad[i, :, place_of(1)] = (k_grad * HD ** (-0.5)).astype(BF)
            proj_grad[i, :, place_of(2)] = v_grad.astype(BF)
            return carry

        lax.fori_loop(0, pairs, pair_step, 0)
        run(steps - 1, 2)
    upstream[...] = sum(
        mm(proj_grad[i, :, which * cols : (which + 1) * cols], w_vmem[i, which], ((1,), (1,)))
        for i in range(2)
        for which in range(3)
    ).astype(BF)
    pack(upstream[...], given_2, maps, whole)
    second = list(zip(given_2, taken_2))
    send_all(second, send_2, recv_2)

    def attend_at(which):
        return pl.ds(pl.multiple_of(which * cols, 128), cols)

    def late_other(which, carry):
        value = mm(buffer[...], proj_grad[1, :, attend_at(which)], ((0,), (0,)))
        late_give[:, attend_at(which)] = value.astype(BF)
        return carry

    def late_own(which, carry):
        value = mm(buffer[...], proj_grad[0, :, attend_at(which)], ((0,), (0,)))
        got = late_got[:, attend_at(which)].astype(F32)
        late_got[:, attend_at(which)] = (value + got).astype(BF)
        return carry

    lax.fori_loop(0, 3, late_other, 0)
    attend_copy.start()
    run(steps - 1, 2)
    attend_copy.wait_recv()
    lax.fori_loop(0, 3, late_own, 0)
    begin(steps)
    run(steps - 1, 4)

    wait_all(second, send_2, recv_2)
    unpack(taken_2, maps, whole, upstream)
    tokens_own = hidden

    def first_rows(r, carry, kept):
        rows = rows_of(r)
        normal, scale = norm_stats(x[rows, :].astype(F32))
        normed = (normal * gain[...] + shift[...]).astype(BF).astype(F32)
        logit = logit_grad[rows, :]
        grad = logit * router[...]
        if kept:
            grad = grad + jnp.where(route_cols[rows, 1:2] > 0.5, upstream[rows, :].astype(F32), 0.0)
        total = mixed_grad[rows, :] + norm_pull(grad * gain[...], normal, scale)
        tokens_own[rows, :] = total.astype(BF)
        return (
            carry[0] + row_sums(grad * normal),
            carry[1] + row_sums(grad),
            carry[2] + row_sums(logit * normed),
        )

    carry = (zeros, zeros, zeros)
    carry = lax.fori_loop(0, kept_steps, functools.partial(first_rows, kept=True), carry)
    carry = lax.fori_loop(kept_steps, all_steps, functools.partial(first_rows, kept=False), carry)
    tokens_copy = pair_copy(2 * steps + 2, tokens_own, tokens_got)
    tokens_copy.start()
    for i in range(3):
        sums[0, i : i + 1, :] = jnp.sum(carry[i], axis=0, keepdims=True)

    def sums_copy(stage):
        if stage < sums_got.shape[0] - 1:
            bit = lax.rem(lax.div(dp, 1 << stage), 2)
            to = (dp + (1 - 2 * bit) * (1 << stage), core)
        else:
            to = (dp, 1 - core)
        return pltpu.make_async_remote_copy(
            src_ref=sums.at[stage],
            dst_ref=sums_got.at[stage],
            send_sem=sums_send.at[stage],
            recv_sem=sums_recv.at[stage],
            device_id=to,
            device_id_type=MESH,
        )

    sums_stages = sums_got.shape[0]
    sums_copy(0).start()

    def sums_step(stage):
        sums_copy(stage).wait_recv()
        total = sums[stage] + sums_got[stage]
        if stage + 1 < sums_stages:
            sums[stage + 1] = total
            sums_copy(stage + 1).start()
        else:
            sums_out[...] = total

    def unpick(own, other, out, stage, sems):
        total = out.shape[0]
        block = stage.shape[1]
        full = total // block
        tail = total - full * block

        def out_copy(r, size):
            slot = lax.rem(r, 2)
            rows = pl.ds(pl.multiple_of(r * block, block), size)
            return pltpu.make_async_copy(
                stage.at[slot, pl.ds(0, size), :], out.at[rows, :], sems.at[slot]
            )

        def emit(r, size):
            rows = pl.ds(pl.multiple_of(r * block, block), size)
            hit = (route_cols[rows, 2:3] == routes[0:1, :]).astype(F32).astype(BF)
            value = mm(hit[:, :count], own[...], ((1,), (0,))) + mm(
                hit[:, count : 2 * count], other[...], ((1,), (0,))
            )
            stage[lax.rem(r, 2), pl.ds(0, size), :] = value.astype(out.dtype)
            out_copy(r, size).start()

        def body(r, carry):
            @pl.when(r >= 2)
            def _():
                out_copy(r - 2, block).wait()

            emit(r, block)
            return carry

        lax.fori_loop(0, full, body, 0)
        if tail:
            out_copy(full - 2, block).wait()
            emit(full, tail)
            out_copy(full - 1, block).wait()
            out_copy(full, tail).wait()
        else:
            out_copy(full - 2, block).wait()
            out_copy(full - 1, block).wait()

    run(steps - 1, 3)
    run(steps, 4)
    sums_step(0)
    layer_copy.wait_recv()
    unpick(layer_own, ct, layer_out, layer_stage, out_sem.at[0])
    sums_step(1)
    run(steps - 1, 15)
    run(steps, 2)
    sums_step(2)
    tokens_copy.wait_recv()
    unpick(tokens_own, tokens_got, tokens_out, tokens_stage, out_sem.at[1])
    sums_step(3)
    run(steps, 2)
    for stage in range(4, sums_stages):
        sums_step(stage)
    run(steps, 15)
    for chain in chains:
        chain.drain()
    if not chains:
        finals = [
            pltpu.make_async_copy(here, there, load_sem.at[i])
            for i, (here, there) in enumerate(
                ((expand_got, expand_out), (reduce_got, reduce_out), (late_got, late_out))
            )
        ]
        for final in finals:
            final.start()
        for final in finals:
            final.wait()
    for copy in (output_copy, attend_copy, layer_copy, tokens_copy):
        copy.wait_send()
    for stage in range(sums_stages):
        sums_copy(stage).wait_send()


def split_blocks(blocks):
    step = len(blocks) // 4
    return [blocks[i * step : (i + 1) * step] for i in range(4)]


def block_scratch(peers, whole, left, parts, width):
    shapes = [(peers, whole, width)] if whole else []
    shapes.append((peers, 16, width // parts))
    return [pltpu.VMEM(shape, BF) for _ in range(4) for shape in shapes], len(shapes)


def exchange_call(
    kernel, name, collective_id, capacity, width, args, spaces, outs, scratch, after=(), out_spaces=None
):
    peers = lax.axis_size("dp")
    whole, left, parts = block_plan(capacity, width)
    blocks, kinds = block_scratch(peers, whole, left, parts, width)
    return pl.pallas_call(
        functools.partial(kernel, whole),
        out_shape=[jax.ShapeDtypeStruct(*out) for out in outs],
        in_specs=[pl.BlockSpec(memory_space=space) for space in spaces],
        out_specs=[
            pl.BlockSpec(memory_space=space) for space in out_spaces or [pltpu.VMEM] * len(outs)
        ],
        scratch_shapes=[
            *scratch,
            *[pltpu.SemaphoreType.DMA((kinds, peers))] * 4,
            *blocks,
            *after,
        ],
        compiler_params=pltpu.CompilerParams(
            collective_id=collective_id, has_side_effects=True, vmem_limit_bytes=58 * 2**20
        ),
        name=name,
    )(*args)


def slot_layout(peers, capacity, whole, own, own_pad, total):
    left = capacity - whole
    spot = np.arange(total) % own_pad
    side = np.arange(total) // own_pad
    main = spot < peers * whole
    rest = spot - peers * whole
    device = np.where(main, spot // max(whole, 1), rest // left)
    slot = np.where(main, spot % max(whole, 1), whole + rest % left)
    is_slot = spot < peers * capacity
    rows = [
        np.where(is_slot, device, 0),
        np.where(is_slot, slot, 4 * capacity),
        np.where((spot < own) & (side < 2), spot, -1),
        np.minimum(side, 1),
    ]
    return jnp.asarray(np.stack(rows + [np.zeros(total)] * 4), jnp.int32)


def attend(info, vectors, maps, tokens, cotangent, w_own, w_other, capacity, own, own_pad):
    peers = lax.axis_size("dp")
    count, width = tokens.shape
    slots = peers * capacity
    cols = w_own.shape[2]
    heads = 2 * cols // HD
    total = info.shape[1]
    whole = block_plan(capacity, width)[0]
    layout = slot_layout(peers, capacity, whole, own, own_pad, total)
    vmem = pltpu.VMEM
    return exchange_call(
        lambda whole, *refs: attend_kernel(whole, capacity, *refs), "attend", 0, capacity, width,
        (info, layout, vectors, maps, tokens, cotangent, w_own, w_other),
        (vmem,) * 4 + (pl.ANY,) * 4,
        [
            ((slots, width), BF), ((slots, width), BF), ((2, slots, 3 * cols), BF),
            ((heads, slots, slots), BF), ((own_pad, width), BF), ((own_pad, width), BF),
            ((own_pad, 1), F32), ((8, total), F32), ((total, 8), F32),
        ],
        [
            vmem((count, width), BF), vmem((count, width), BF),
            vmem((total, 8), F32), vmem((8, total), F32),
            vmem((2, *w_own.shape), BF),
            vmem((slots, width), BF),
            vmem((8, slots), F32),
            pltpu.SemaphoreType.DMA((4,)),
        ],
    )


def back(small, large, probs, capacity, orders, place_rows):
    gathered, wo, _, x, ct, we, _, wr, _, w, _, proj, _, buffer = large
    slots, width = buffer.shape
    count, hidden = x.shape[0], we.shape[1]
    peers = lax.axis_size("dp")
    vmem, hbm = pltpu.VMEM, pl.ANY
    dma = pltpu.SemaphoreType.DMA
    chunk = 512 if hidden % 512 == 0 else hidden
    steps = hidden // chunk
    rows = width // peers
    after = []
    if orders is None:
        outs = [((width, hidden), BF)] * 3
        out_spaces = (hbm,) * 5 + (vmem,)
    else:
        outs = [((rows, hidden), F32)] * 3
        out_spaces = (vmem,) * 3 + (hbm,) * 2 + (vmem,)
        counts = [peers >> (stage + 1) for stage in range(len(orders[0]))]
        for size in [chunk] * (2 * steps) + [hidden // 2] * 2:
            after += [dma((sum(counts),))] * 2
            after += [vmem((n, rows, size), BF) for n in counts]
    outs += [((place_rows, width), BF), ((place_rows, width), F32), ((8, width), F32)]
    sums_stages = peers.bit_length()
    low = vmem((count, width), BF)
    wide = vmem((count, width), F32)
    turned = vmem((width, count), BF)
    column = vmem((count, 1), F32)
    slot_rows = vmem((slots, width), BF)
    gradient = vmem((width, hidden), BF)
    return exchange_call(
        lambda whole, *refs: back_kernel(whole, orders, *refs), "back", 1, capacity, width,
        (*small, *large),
        (vmem,) * len(small) + (hbm,) * len(large),
        outs,
        [
            slot_rows, vmem((2, *wo.shape), BF), low, low, vmem((2, *w.shape), BF),
            vmem(proj.shape, BF), vmem(probs.shape, BF), slot_rows,
            vmem((2, width, chunk), BF), vmem((2, chunk, width), BF),
            vmem((slots, width), F32), column, column, low, turned, turned, wide, wide,
            vmem((count, chunk), F32), vmem((count, chunk), F32),
            vmem((count, chunk), BF), vmem((count, chunk), BF),
            column, slot_rows, slot_rows, vmem(proj.shape, BF), low, low,
            gradient, gradient, gradient, gradient,
            vmem((sums_stages, 8, width), F32), vmem((sums_stages, 8, width), F32),
            vmem((2, 128, width), BF), vmem((2, 128, width), F32),
            dma((10,)), dma((2,)), dma((2,)), dma((2, 2)),
            dma((2 * steps + 4,)), dma((2 * steps + 4,)), dma((sums_stages,)), dma((sums_stages,)),
            pltpu.SemaphoreType.REGULAR,
        ],
        after,
        out_spaces,
    )


def shards(
    tokens,
    row_ids,
    select,
    priority,
    first_gain,
    first_shift,
    router,
    w_attend,
    w_output,
    second_gain,
    second_shift,
    w_expand,
    w_reduce,
    cotangent,
):
    dp_count = lax.axis_size("dp")
    mp_count = lax.axis_size("mp")
    core = lax.axis_index("mp")
    bits = dp_count.bit_length() - 1
    order_a = list(range(bits))
    order_b = [1, 0] + list(range(bits - 1, 1, -1))
    capacity = 5 * ROW_LEN // (8 * dp_count)
    count, width = tokens.shape
    own = count // mp_count
    own_pad = -(-own // 128) * 128
    heads_cols = w_attend.shape[2]
    whole, left, parts = block_plan(capacity, width)
    maps = rest_map(dp_count, left, parts)

    w_attend = w_attend.transpose(1, 0, 2)
    w_attend_2 = (w_attend, swap(w_attend))
    w_output_2 = (w_output, swap(w_output))
    w_expand_2 = (w_expand, swap(w_expand))
    w_reduce_2 = (w_reduce, swap(w_reduce))

    total = max(-(-count // 128) * 128, mp_count * own_pad)
    info = jnp.pad(jnp.stack([row_ids, select, priority]), ((0, 5), (0, total - count)))
    vectors = jnp.pad(
        jnp.stack([first_gain, first_shift, router, second_gain, second_shift]), ((0, 3), (0, 0))
    )
    gathered, buffer, proj, probs, x, ct, gate, routes, route_cols = attend(
        info, vectors, maps, tokens, cotangent, *w_attend_2, capacity, own, own_pad
    )
    orders = (order_a, order_b) if width // dp_count % 16 == 0 else None
    expand_sum, reduce_sum, late_sum, layer_out, tokens_grad, vectors = back(
        (maps, gate, vectors, routes, route_cols),
        (gathered, *w_output_2, x, ct, *w_expand_2, *w_reduce_2, *w_attend_2, proj, probs, buffer),
        probs, capacity, orders, -(-count // 16) * 16,
    )
    if orders is None:
        expand_sum = scatter_sum(expand_sum, order_a)
        reduce_sum = scatter_sum(reduce_sum, order_b)
        late_sum = scatter_sum(late_sum, order_a)
    rows_here = width // dp_count
    vectors = lax.dynamic_slice_in_dim(vectors, lax.axis_index("dp") * rows_here, rows_here, 1)

    attend_cols = 3 * heads_cols
    return (
        layer_out[:count],
        tokens_grad[:count],
        vectors[0],
        vectors[1],
        vectors[2],
        late_sum[:, :attend_cols].reshape(-1, 3, heads_cols),
        late_sum[:, attend_cols:].T,
        vectors[3],
        vectors[4],
        expand_sum,
        reduce_sum.T,
    )


def solution(mesh):
    in_specs = (
        P("dp", None),
        P("dp"),
        P("dp"),
        P("dp"),
        P(),
        P(),
        P(),
        P(None, None, "mp"),
        P("mp", None),
        P(),
        P(),
        P(None, "mp"),
        P("mp", None),
        P("dp", None),
    )
    out_specs = (
        P("dp", None),
        P("dp", None),
        P("dp"),
        P("dp"),
        P("dp"),
        P("dp", None, "mp"),
        P("mp", "dp"),
        P("dp"),
        P("dp"),
        P("dp", "mp"),
        P("mp", "dp"),
    )
    return jax.shard_map(shards, mesh=mesh, in_specs=in_specs, out_specs=out_specs, check_vma=False)
```

time: 250 us -> 216 us (0.86); the launches traced: 245 us -> 216 us
  Pallas kernels: 204 us -> 192 us
  other arithmetic: 11.9 us -> 0.99 us
  matrix products: 5.52 us -> 0 us
    pallas_call x1 -> x0, Pallas kernels: 49.3 us -> none  [feed(): pl.pallas_call(feed_kernel, out_shape=[jax.ShapeDtypeStruct(shape, kind)...]
    pallas_call x2, Pallas kernels: 154 us -> 192 us  [exchange_call(): pl.pallas_call(functools.partial(kernel, whole), out_shape=[jax.ShapeDtyp...]
    reduce_sum x5 -> x0, other arithmetic: 5.88 us -> none  [the longest x1 2.65 us: shards(): jnp.sum((same_row & earlier & chosen[None, :]).astype(jnp.int32), axis=1)]
    dot_general x2 -> x0, matrix products: 5.52 us -> none  [mm(): return lax.dot_general(a, b, (dims, ((), ())), preferred_element_type=F32)]
    another operation x4 -> x9, local copies, waits for them, and re-layouts: 0.31 us -> 5.59 us  [the longest x6 3.48 us: shards(): jnp.stack([first_gain, first_shift, router, second_gain, second_shift])]
    unnamed x38 -> x12, local copies, waits for them, and re-layouts: 7.71 us -> 3.43 us
    select_n x9 -> x0, other arithmetic: 3.49 us -> none  [the longest x1 1.97 us: shards(): jnp.where(mask, normed[:slots], jnp.asarray(EMPTY, BF))]
    broadcast_in_dim x7 -> x0, local copies, waits for them, and re-layouts: 3.44 us -> none  [the longest x2 1.17 us: shards(): normed = (nhat_1 * first_gain + first_shift).astype(BF)]
  transfers between devices with their start and end apart: 4 -> 4, of which waited for: 0 -> 1; matrix products, arithmetic and copies ran while one was open for 9% -> 4% of each run, Pallas kernels for 17% -> 23%
where the time goes in v1:
time: 216 us
  Pallas kernels  192 us (89%)
  local copies, waits for them, and re-layouts  20.2 us (9%)
    pallas_call x2, Pallas kernels, exchange_call(): pl.pallas_call(functools.partial(kernel, whole), out_shape=[jax.ShapeDtyp...  192 us
  transfers between devices with their start and end apart: 4, of which 1 were waited for; matrix products, arithmetic and copies ran while one was open for 4% of the time, Pallas kernels for 23%

profile of v1, /device:TPU:0, one launch (start us, length us, event | category | flops | bytes accessed | tf_op | source)
XLA Modules:
  0.0 215.9 jit_solution(16933794122906132808)
XLA Ops:
  0.6 0.5 collective-permute-start.2
  1.2 0.1 collective-permute-start.3
  1.2 0.4 collective-permute-start
  1.7 0.1 collective-permute-start.1
  1.8 0.7 stack.30
  2.5 0.7 stack.31
  3.2 0.7 stack.32
  3.9 0.1 broadcast_add_fusion
  4.0 0.7 stack.34
  4.7 0.7 stack.35
  5.4 0.7 stack.36
  6.1 0.7 stack.37
  6.8 0.7 stack.38
  7.4 0.6 pad.8.refs_0_
  8.1 0.6 pad.9.refs_2_
  8.7 0.1 broadcast_compare_fusion
  8.8 0.8 and_convert_fusion.refs_3_.refs_0_
  9.6 1.0 collective-permute-done.refs_7_.refs_15_
  10.6 0.0 copy-start
  10.6 1.2 copy-done
  11.8 49.8 %attend.1 = (bf16[352,768]{1,0:T(8,128)(2,1)}, bf16[352,768]{1,0:T(8,128)(2,1)}, bf16[2,352,1152]{2,1,0:T(8,128)(2,1)}, bf16[12,352,352]{2,1,0:T(8,128)(2,1)}, b...) custom-call(s32[8,1280]{1,0:T(8,128)} %pad.8.refs_0_, ...), custom_call_target="tpu_custom_call" | custom-call | tf_op jit(solution)/shard_map/attend/pallas_call | solution.py:889
  61.6 0.0 collective-permute-done.1.refs_7_
  61.6 0.0 copy-start.2
  61.7 0.0 collective-permute-done.2.refs_11_
  61.7 0.0 collective-permute-done.3.refs_13_
  61.7 0.8 copy-done.2
  62.5 142.0 %back.1 = (f32[48,1536]{1,0:T(8,128)}, f32[48,1536]{1,0:T(8,128)}, f32[48,1536]{1,0:T(8,128)}, bf16[1168,768]{1,0:T(8,128)(2,1)}, f32[1168,768]{1,0:T(8,128)}, /*index=5*/f32[8,768]{1,0:T(8,128)}) custom-call(bf16[2,256,96]{2,1,0:T(8,128)(2,1)} %and_convert_fusion.refs_3_.refs_0_, f32[640,1]{1,0:T(8,128)} %get-tuple-element.26.refs_1_, ...), custom_call_target="tpu_custom_call" | custom-call | tf_op jit(solution)/shard_map/back/pallas_call | solution.py:889
  204.5 1.0 slice.32
  205.5 1.5 slice_bitcast_fusion
  207.0 0.0 copy-start.1
  207.0 4.2 %slice.28 = f32[1154,768]{1,0:T(8,128)} slice(f32[1168,768]{1,0:T(8,128)} %get-tuple-element.36), slice={[0:1154], [0:768]} | slice | bytes 7090176 | tf_op jit(solution)/shard_map/slice | solution.py:1071
  211.2 0.0 copy-start.4
  211.2 0.0 copy-start.3
  211.2 0.0 copy-done.1
  211.2 1.3 slice.27
  212.5 0.7 copy.30
  213.2 0.8 constant_dynamic-slice_fusion
  214.0 0.5 slice_bitcast_fusion.1
  214.5 0.0 copy-done.4
  214.5 0.7 copy.33
  215.2 0.0 copy-done.3
  215.2 0.7 copy.34
  (7 shorter events, 0.1 us)
Async XLA Ops:
  0.6 61.0 %collective-permute-start.2 = (bf16[768,1536]{1,0:T(8,128)(2,1)}, bf16[768,1536]{1,0:T(8,128)(2,1)}, u32[]{:S(2)}, u32[]{:S(2)}) collective-permute-start(bf16[768,1536]{1,0:T(8,128)(2,1)} %refs_10_.1), channel_id=1, source_target_pairs={{0,1},{1,0},{2,3},{3,2},{4,5},{5,4},{6,7},{7,6},{8,9},{9,8},{10,11... | collective-permute-start | bytes 7077896 | tf_op jit(solution)/shard_map/ppermute | solution.py:36
  1.2 60.5 %collective-permute-start.3 = (bf16[1536,768]{1,0:T(8,128)(2,1)}, bf16[1536,768]{1,0:T(8,128)(2,1)}, u32[]{:S(2)}, u32[]{:S(2)}) collective-permute-start(bf16[1536,768]{1,0:T(8,128)(2,1)} %refs_12_.1), channel_id=1, source_target_pairs={{0,1},{1,0},{2,3},{3,2},{4,5},{5,4},{6,7},{7,6},{8,9},{9,8},{10,11... | collective-permute-start | bytes 7077896 | tf_op jit(solution)/shard_map/ppermute | solution.py:36
  1.2 9.4 %collective-permute-start = (bf16[3,768,384]{2,1,0:T(8,128)(2,1)}, bf16[3,768,384]{2,1,0:T(8,128)(2,1)S(1)}, u32[]{:S(2)}, u32[]{:S(2)}) collective-permute-start(bf16[3,768,384]{2,1,0:T(8,128)(2,1)} %bitcast.18), channel_id=1, source_target_pairs={{0,1},{1,0},{2,3},{3,2},{4,5},{5,4},{6,7},{7,6},{8,9},{9,8},{10,11... | collective-permute-start | bytes 5308424 | tf_op jit(solution)/shard_map/ppermute | solution.py:36
  1.7 60.0 %collective-permute-start.1 = (bf16[384,768]{1,0:T(8,128)(2,1)}, bf16[384,768]{1,0:T(8,128)(2,1)S(1)}, u32[]{:S(2)}, u32[]{:S(2)}) collective-permute-start(bf16[384,768]{1,0:T(8,128)(2,1)} %refs_6_.1), channel_id=1, source_target_pairs={{0,1},{1,0},{2,3},{3,2},{4,5},{5,4},{6,7},{7,6},{8,9},{9,8},{10,11... | collective-permute-start | bytes 1769480 | tf_op jit(solution)/shard_map/ppermute | solution.py:36
  10.6 1.2 copy-start
  61.6 0.8 copy-start.2
  207.0 4.2 %copy-start.1 = (bf16[1168,768]{1,0:T(8,128)(2,1)S(1)}, bf16[1168,768]{1,0:T(8,128)(2,1)}, u32[]{:S(2)}) copy-start(bf16[1168,768]{1,0:T(8,128)(2,1)} %get-tuple-element.35) | copy-start | bytes 5382148
  211.2 3.3 %copy-start.4 = (f32[48,1536]{1,0:T(8,128)S(1)}, f32[48,1536]{1,0:T(8,128)}, u32[]{:S(2)}) copy-start(f32[48,1536]{1,0:T(8,128)} %get-tuple-element.88) | copy-start | bytes 884740
  211.2 4.1 %copy-start.3 = (f32[48,1536]{1,0:T(8,128)S(1)}, f32[48,1536]{1,0:T(8,128)}, u32[]{:S(2)}) copy-start(f32[48,1536]{1,0:T(8,128)} %get-tuple-element.40) | copy-start | bytes 884740
